TPU v7x, 256 devices: a whole 4x4x8 slice. The times are simulated.
256 devices in a mesh: sec: 16 (over x, z_hi, core), tile: 16 (over y, z_lo).
Axes of the slice: x: 4, y: 4, z: 8 (z_hi: 2, z_lo: 4; z = z_hi * 4 + z_lo), core: 2. Of those that a mesh axis runs over, the one named last changes fastest.
Arguments:
- sections: float32 [16, 16, 256, 512], P('sec', 'tile'), may hold values from -41 to 41
- following: float32 [16, 448, 704], P('tile'), may hold values from -41 to 41, as said below
Outputs:
- flow: float32 [16, 16, 2, 32], P('sec', 'tile')
- strength: float32 [16, 16, 32], P('sec', 'tile')
Inputs may be any that keep to these rules, and one draw needn't show every extreme that they name: `following`: tile t = 4 * r + c holds the 448 by 512 + 3 * 64 cells of that section from row 256 * r - 96 and column 512 * c - 96, with 0 outside the section.
All inputs are finite; a program needn't handle non-finite values.
Results may differ from a plain program's by a relative error of at most 0.029.
Values sent between devices are 32-bit elements; how exact they have to be, the bound alone decides.
A program may use at most 64 MiB of HBM per device.

v0:
```python
import math

import jax
import jax.numpy as jnp
from jax import lax
from jax.sharding import PartitionSpec as P

PATCH = 128
TCOLS = 4


sharpness = 128.0


def passed_along(value, axis, steps):
    count = lax.axis_size(axis)
    leading, last = (max(0, -steps), min(count, count - steps))
    return lax.ppermute(value, axis, [(source, source + steps) for source in range(leading, last)])


def spectral_tables(length):
    counter = jnp.arange(length, dtype=jnp.int32)
    turn_index = counter[:, None] * counter[None, :] % length
    phase_angle = turn_index.astype(jnp.float32) * (2.0 * math.pi / length)
    return (jnp.cos(phase_angle).astype(jnp.bfloat16), jnp.sin(phase_angle).astype(jnp.bfloat16))


def narrow_product(left_matrix, operand):
    return jnp.einsum("ki,bim->bkm", left_matrix, operand, preferred_element_type=jnp.float32)


def split_spectrum(product, length):
    cos_cos = product[:, :length, :length]
    cos_sin = product[:, :length, length:]
    sin_cos = product[:, length:, :length]
    sin_sin = product[:, length:, length:]
    return ((cos_cos - sin_sin).astype(jnp.bfloat16), (-(sin_cos + cos_sin)).astype(jnp.bfloat16))


def spectrum(images, extent, cos_t, sin_t, multiply):
    batch_size = images.shape[0]
    length = cos_t.shape[0]
    right_table = jnp.concatenate([cos_t[:extent], sin_t[:extent]], 1)
    segment_one = jnp.dot(
        images.reshape(batch_size * extent, extent), right_table, preferred_element_type=jnp.float32
    )
    segment_one = segment_one.astype(jnp.bfloat16).reshape(batch_size, extent, 2 * length)
    left_table = jnp.concatenate([cos_t[:, :extent], sin_t[:, :extent]], 0)
    return split_spectrum(multiply(left_table, segment_one), length)


def soft_peak(scores, extent):
    highest = jnp.max(scores, axis=(1, 2), keepdims=True)
    weight = jnp.exp(scores - highest)
    weight_sum = jnp.sum(weight, axis=(1, 2))
    offset = jnp.arange(extent, dtype=jnp.float32) - float(extent // 2)
    by_row = jnp.sum(weight, axis=2)
    by_col = jnp.sum(weight, axis=1)
    flow_rows = jnp.sum(by_row * offset, axis=1) / weight_sum
    flow_cols = jnp.sum(by_col * offset, axis=1) / weight_sum
    strength = (highest[:, 0, 0] + jnp.log(weight_sum)) / sharpness
    return (jnp.stack([flow_rows, flow_cols], 1), strength)


def correlate(patches, windows, multiply):
    batch_size = windows.shape[0]
    length = windows.shape[1]
    extent = patches.shape[1]
    cos_t, sin_t = spectral_tables(length)
    win_real, win_imag = spectrum(windows, length, cos_t, sin_t, multiply)
    pat_real, pat_imag = spectrum(patches, extent, cos_t, sin_t, multiply)
    pr32 = pat_real.astype(jnp.float32)
    pi32 = pat_imag.astype(jnp.float32)
    wr32 = win_real.astype(jnp.float32)
    wi32 = win_imag.astype(jnp.float32)
    cross_real = (pr32 * wr32 + pi32 * wi32).astype(jnp.bfloat16)
    cross_imag = (pr32 * wi32 - pi32 * wr32).astype(jnp.bfloat16)
    mixing = jnp.concatenate(
        [
            jnp.concatenate([cos_t[:, :extent], sin_t[:, :extent]], 1),
            jnp.concatenate([-sin_t[:, :extent], cos_t[:, :extent]], 1),
        ],
        0,
    )
    joined = jnp.concatenate([cross_real, cross_imag], 2).reshape(batch_size * length, 2 * length)
    returned = jnp.dot(joined, mixing, preferred_element_type=jnp.float32)
    returned = returned.astype(jnp.bfloat16).reshape(batch_size, length, 2 * extent)
    stacked = jnp.concatenate([returned[:, :, :extent], returned[:, :, extent:]], 1)
    final_table = jnp.concatenate([cos_t[:extent], -sin_t[:extent]], 1)
    correlation = multiply(final_table, stacked)
    scores = correlation * (sharpness / float(length * length * extent * extent))
    return soft_peak(scores, extent)


def standardize(images):
    centre = jnp.mean(images, axis=(1, 2), keepdims=True)
    deviation = images - centre
    spread = jnp.mean(deviation * deviation, axis=(1, 2), keepdims=True)
    return (deviation * lax.rsqrt(spread + 1e-05)).astype(jnp.bfloat16)


def cut_patches(strip_cells, extent, stride, batch_size):
    block_span = extent // stride
    blocks = strip_cells.reshape(extent, batch_size + block_span - 1, stride)
    gathered = jnp.concatenate(
        [blocks[:, lead_block : lead_block + batch_size] for lead_block in range(block_span)], 2
    )
    return gathered.transpose(1, 0, 2)


def extend_rims(source, margin, mover, grid_row, grid_col, grid_rows):

    def fetch(step_row, step_col):
        rows_part = (
            source[-margin:] if step_row < 0 else source[:margin] if step_row > 0 else source
        )
        portion = (
            rows_part[:, -margin:]
            if step_col < 0
            else rows_part[:, :margin] if step_col > 0 else rows_part
        )
        arrived = mover(portion, -(step_row * TCOLS + step_col))
        inside = (
            (grid_row + step_row >= 0)
            & (grid_row + step_row < grid_rows)
            & (grid_col + step_col >= 0)
            & (grid_col + step_col < TCOLS)
        )
        return jnp.where(inside, arrived, jnp.zeros_like(arrived))

    upper_band = jnp.concatenate([fetch(-1, -1), fetch(-1, 0), fetch(-1, 1)], 1)
    middle_band = jnp.concatenate([fetch(0, -1), source, fetch(0, 1)], 1)
    lower_band = jnp.concatenate([fetch(1, -1), fetch(1, 0), fetch(1, 1)], 1)
    return jnp.concatenate([upper_band, middle_band, lower_band], 0)


def local(sections, following):
    own_tile = sections[0, 0]
    spare_tile = following[0]
    stride = PATCH // 2
    own_margin = PATCH // 4
    next_margin = 3 * PATCH // 4
    window = 2 * PATCH
    grid_rows = lax.axis_size("tile") // TCOLS
    tile_place = lax.axis_index("tile")
    grid_row = tile_place // TCOLS
    grid_col = tile_place % TCOLS
    final_sec = lax.axis_index("sec") == lax.axis_size("sec") - 1
    arriving = passed_along(own_tile, "sec", -1)
    own_ext = extend_rims(
        own_tile,
        own_margin,
        lambda source, offset: passed_along(source, "tile", offset),
        grid_row,
        grid_col,
        grid_rows,
    )
    next_ext = extend_rims(
        arriving,
        next_margin,
        lambda source, offset: passed_along(source, "tile", offset),
        grid_row,
        grid_col,
        grid_rows,
    )
    next_ext = jnp.where(final_sec, spare_tile, next_ext)
    patch_rows = own_tile.shape[0] // stride
    patch_cols = own_tile.shape[1] // stride
    group_count = patch_cols // 4

    def one_group(group_index):
        band_row = group_index // group_count * stride
        column_start = group_index % group_count * (4 * stride)
        own_strip = lax.dynamic_slice(own_ext, (band_row, column_start), (PATCH, 5 * stride))
        next_strip = lax.dynamic_slice(next_ext, (band_row, column_start), (window, 7 * stride))
        patches = standardize(cut_patches(own_strip, PATCH, stride, 4))
        windows = standardize(cut_patches(next_strip, window, stride, 4))
        return correlate(patches, windows, narrow_product)

    flow_out, strength = lax.map(one_group, jnp.arange(patch_rows * group_count, dtype=jnp.int32))
    flow_out = flow_out.reshape(patch_rows * patch_cols, 2).transpose(1, 0)
    strength = strength.reshape(patch_rows * patch_cols)
    return (flow_out[None, None], strength[None, None])


def solution(mesh):
    placed = (P("sec", "tile", None, None), P("tile", None, None))
    return jax.shard_map(
        local,
        mesh=mesh,
        in_specs=placed,
        out_specs=(P("sec", "tile", None, None), P("sec", "tile", None)),
        check_vma=False,
    )
```

profile of v0, /device:TPU:22, one launch (start us, length us, event | category | flops | bytes accessed | tf_op | source)
XLA Modules:
  0.0 252.9 jit_solution(12281117773850236931)
XLA Ops:
  0.6 1.2 copy.40
  1.9 8.8 %collective-permute-start.8 = (f32[256,512]{0,1:T(8,128)S(1)}, f32[256,512]{0,1:T(8,128)S(1)}, u32[]{:S(2)}, u32[]{:S(2)}) collective-permute-start(f32[256,512]{0,1:T(8,128)S(1)} %bitcast.108), channel_id=1, source_target_pairs={{16,0},{32,16},{48,32},{64,48},{80,64},{96,80},{112,96},{128,112},... | collective-permute-start | bytes 1572872 | tf_op jit(solution)/shard_map/ppermute | solution.py:18
  11.6 3.2 %collective-permute-start.1 = (f32[32,512]{1,0:T(8,128)S(1)}, f32[32,512]{1,0:T(8,128)S(1)}, u32[]{:S(2)}, u32[]{:S(2)}) collective-permute-start(f32[32,512]{1,0:T(8,128)S(1)} %get-tuple-element.170), channel_id=1, source_target_pairs={{0,4},{1,5},{2,6},{3,7},{4,8},{5,9},{6,10},{7,11},{8,12},{9,13},{1... | collective-permute-start | bytes 196616 | tf_op jit(solution)/shard_map/ppermute | solution.py:18
  14.8 3.8 %collective-permute-start.2 = (f32[32,32]{1,0:T(8,128)S(1)}, f32[32,32]{1,0:T(8,128)S(1)}, u32[]{:S(2)}, u32[]{:S(2)}) collective-permute-start(f32[32,32]{1,0:T(8,128)S(1)} %get-tuple-element.175), channel_id=1, source_target_pairs={{0,3},{1,4},{2,5},{3,6},{4,7},{5,8},{6,9},{7,10},{8,11},{9,12},{10... | collective-permute-start | bytes 12296 | tf_op jit(solution)/shard_map/ppermute | solution.py:18
  18.7 1.9 collective-permute-start
  20.6 2.5 collective-permute-start.6
  23.2 1.8 copy.43
  25.2 8.0 %collective-permute-start.4 = (f32[256,32]{0,1:T(8,128)S(1)}, f32[256,32]{0,1:T(8,128)S(1)}, u32[]{:S(2)}, u32[]{:S(2)}) collective-permute-start(f32[256,32]{0,1:T(8,128)S(1)} %get-tuple-element.173), channel_id=1, source_target_pairs={{1,0},{2,1},{3,2},{4,3},{5,4},{6,5},{7,6},{8,7},{9,8},{10,9},{11,1... | collective-permute-start | bytes 98312 | tf_op jit(solution)/shard_map/ppermute | solution.py:18
  33.2 1.9 collective-permute-start.5
  35.2 5.5 %collective-permute-done.5 = f32[32,32]{1,0:T(8,128)S(1)} collective-permute-done((f32[32,32]{1,0:T(8,128)S(1)}, f32[32,32]{1,0:T(8,128)S(1)}, u32[]{:S(2)}, u32[]{:S(2)}) %collective-permute-start.5) | collective-permute-done | bytes 4128 | tf_op jit(solution)/shard_map/ppermute | solution.py:18
  40.6 1.9 collective-permute-start.7
  42.6 4.6 %collective-permute-done.7 = f32[32,32]{1,0:T(8,128)S(1)} collective-permute-done((f32[32,32]{1,0:T(8,128)S(1)}, f32[32,32]{1,0:T(8,128)S(1)}, u32[]{:S(2)}, u32[]{:S(2)}) %collective-permute-start.7) | collective-permute-done | bytes 4128 | tf_op jit(solution)/shard_map/ppermute | solution.py:18
  47.2 1.9 collective-permute-start.3
  49.1 6.5 %collective-permute-done.3 = f32[256,32]{0,1:T(8,128)S(1)} collective-permute-done((f32[256,32]{0,1:T(8,128)S(1)}, f32[256,32]{0,1:T(8,128)S(1)}, u32[]{:S(2)}, u32[]{:S(2)}) %collective-permute-start.3) | collective-permute-done | bytes 32800 | tf_op jit(solution)/shard_map/ppermute | solution.py:18
  56.2 1.3 pad_maximum_fusion.5
  57.7 1.9 collective-permute-start.15
  59.6 3.9 %collective-permute-start.10 = (f32[96,512]{0,1:T(8,128)S(1)}, f32[96,512]{0,1:T(8,128)S(1)}, u32[]{:S(2)}, u32[]{:S(2)}) collective-permute-start(f32[96,512]{0,1:T(8,128)S(1)} %get-tuple-element.166), channel_id=1, source_target_pairs={{0,4},{1,5},{2,6},{3,7},{4,8},{5,9},{6,10},{7,11},{8,12},{9,13},{1... | collective-permute-start | bytes 589832 | tf_op jit(solution)/shard_map/ppermute | solution.py:18
  63.6 1.9 collective-permute-start.14
  65.6 5.2 %collective-permute-start.13 = (f32[256,96]{0,1:T(8,128)S(1)}, f32[256,96]{0,1:T(8,128)S(1)}, u32[]{:S(2)}, u32[]{:S(2)}) collective-permute-start(f32[256,96]{0,1:T(8,128)S(1)} %get-tuple-element.169), channel_id=1, source_target_pairs={{1,0},{2,1},{3,2},{4,3},{5,4},{6,5},{7,6},{8,7},{9,8},{10,9},{11,1... | collective-permute-start | bytes 294920 | tf_op jit(solution)/shard_map/ppermute | solution.py:18
  70.7 1.9 collective-permute-start.12
  72.7 7.2 %collective-permute-start.11 = (f32[96,96]{0,1:T(8,128)S(1)}, f32[96,96]{0,1:T(8,128)S(1)}, u32[]{:S(2)}, u32[]{:S(2)}) collective-permute-start(f32[96,96]{0,1:T(8,128)S(1)} %get-tuple-element.165), channel_id=1, source_target_pairs={{0,3},{1,4},{2,5},{3,6},{4,7},{5,8},{6,9},{7,10},{8,11},{9,12},{10... | collective-permute-start | bytes 110600 | tf_op jit(solution)/shard_map/ppermute | solution.py:18
  79.9 1.7 collective-permute-done.11
  81.6 1.9 collective-permute-start.9
  83.5 8.2 %collective-permute-done.9 = f32[96,96]{0,1:T(8,128)S(1)} collective-permute-done((f32[96,96]{0,1:T(8,128)S(1)}, f32[96,96]{0,1:T(8,128)S(1)}, u32[]{:S(2)}, u32[]{:S(2)}) %collective-permute-start.9) | collective-permute-done | bytes 36896 | tf_op jit(solution)/shard_map/ppermute | solution.py:18
  91.8 1.9 collective-permute-start.16
  93.7 4.9 %collective-permute-done.16 = f32[96,96]{0,1:T(8,128)S(1)} collective-permute-done((f32[96,96]{0,1:T(8,128)S(1)}, f32[96,96]{0,1:T(8,128)S(1)}, u32[]{:S(2)}, u32[]{:S(2)}) %collective-permute-start.16) | collective-permute-done | bytes 36896 | tf_op jit(solution)/shard_map/ppermute | solution.py:18
  99.4 152.3 %while.15 = (s32[]{:T(128)}, f32[8,4,2]{1,0,2:T(8,128)S(1)}, f32[8,4]{1,0:T(8,128)S(1)}, s32[8]{0:T(128)S(1)}, f32[320,576]{0,1:T(8,128)}, /*index=5*/f32[448,70...) while((s32[]{:T(128)}, f32[8,4,2]{1,0,2:T(8,128)S(1)}, ...), condition=%wide.region_15.16_spmd, body=%wide.region_0.15_spmd.sunk | while | flops 1495794816 | bytes 63318432 | solution.py:180
  103.7 1.1 sine_convert_fusion.2
  105.3 2.7 %convolution_bitcast_fusion.5 = f32[4,512,512]{1,2,0:T(8,128)} fusion(bf16[4,256,512]{2,1,0:T(8,128)(2,1)S(1)} %bitcast.101, bf16[256,256]{1,0:T(8,128)(2,1)S(1)} %get-tuple-element.251, bf16[256,256]{1,0:T(8,128)(2,1)S(1)} %get-tuple-element.250), kind=kOutput, calls=%fused_computation.clone.1 | convolution fusion | flops 537395200 | bytes 5505024 | tf_op jit(solution)/shard_map/while/body/eval_jaxpr/ki,bim->bkm/dot_general | solution.py:29
  108.0 1.1 dynamic_slice.26
  112.0 1.5 copy-done
  115.2 1.4 convolution_convert_fusion.8
  122.7 1.1 sine_convert_fusion.2
  124.3 2.7 %convolution_bitcast_fusion.5 = f32[4,512,512]{1,2,0:T(8,128)} fusion(bf16[4,256,512]{2,1,0:T(8,128)(2,1)S(1)} %bitcast.101, bf16[256,256]{1,0:T(8,128)(2,1)S(1)} %get-tuple-element.251, bf16[256,256]{1,0:T(8,128)(2,1)S(1)} %get-tuple-element.250), kind=kOutput, calls=%fused_computation.clone.1 | convolution fusion | flops 537395200 | bytes 5505024 | tf_op jit(solution)/shard_map/while/body/eval_jaxpr/ki,bim->bkm/dot_general | solution.py:29
  127.0 1.1 dynamic_slice.26
  131.0 1.5 copy-done
  134.2 1.4 convolution_convert_fusion.8
  141.8 1.1 sine_convert_fusion.2
  143.3 2.7 %convolution_bitcast_fusion.5 = f32[4,512,512]{1,2,0:T(8,128)} fusion(bf16[4,256,512]{2,1,0:T(8,128)(2,1)S(1)} %bitcast.101, bf16[256,256]{1,0:T(8,128)(2,1)S(1)} %get-tuple-element.251, bf16[256,256]{1,0:T(8,128)(2,1)S(1)} %get-tuple-element.250), kind=kOutput, calls=%fused_computation.clone.1 | convolution fusion | flops 537395200 | bytes 5505024 | tf_op jit(solution)/shard_map/while/body/eval_jaxpr/ki,bim->bkm/dot_general | solution.py:29
  146.0 1.1 dynamic_slice.26
  150.0 1.5 copy-done
  153.3 1.4 convolution_convert_fusion.8
  160.8 1.1 sine_convert_fusion.2
  162.3 2.7 %convolution_bitcast_fusion.5 = f32[4,512,512]{1,2,0:T(8,128)} fusion(bf16[4,256,512]{2,1,0:T(8,128)(2,1)S(1)} %bitcast.101, bf16[256,256]{1,0:T(8,128)(2,1)S(1)} %get-tuple-element.251, bf16[256,256]{1,0:T(8,128)(2,1)S(1)} %get-tuple-element.250), kind=kOutput, calls=%fused_computation.clone.1 | convolution fusion | flops 537395200 | bytes 5505024 | tf_op jit(solution)/shard_map/while/body/eval_jaxpr/ki,bim->bkm/dot_general | solution.py:29
  165.0 1.1 dynamic_slice.26
  169.1 1.5 copy-done
  172.3 1.4 convolution_convert_fusion.8
  179.8 1.1 sine_convert_fusion.2
  181.4 2.7 %convolution_bitcast_fusion.5 = f32[4,512,512]{1,2,0:T(8,128)} fusion(bf16[4,256,512]{2,1,0:T(8,128)(2,1)S(1)} %bitcast.101, bf16[256,256]{1,0:T(8,128)(2,1)S(1)} %get-tuple-element.251, bf16[256,256]{1,0:T(8,128)(2,1)S(1)} %get-tuple-element.250), kind=kOutput, calls=%fused_computation.clone.1 | convolution fusion | flops 537395200 | bytes 5505024 | tf_op jit(solution)/shard_map/while/body/eval_jaxpr/ki,bim->bkm/dot_general | solution.py:29
  184.1 1.1 dynamic_slice.26
  188.1 1.5 copy-done
  191.3 1.4 convolution_convert_fusion.8
  198.9 1.1 sine_convert_fusion.2
  200.4 2.7 %convolution_bitcast_fusion.5 = f32[4,512,512]{1,2,0:T(8,128)} fusion(bf16[4,256,512]{2,1,0:T(8,128)(2,1)S(1)} %bitcast.101, bf16[256,256]{1,0:T(8,128)(2,1)S(1)} %get-tuple-element.251, bf16[256,256]{1,0:T(8,128)(2,1)S(1)} %get-tuple-element.250), kind=kOutput, calls=%fused_computation.clone.1 | convolution fusion | flops 537395200 | bytes 5505024 | tf_op jit(solution)/shard_map/while/body/eval_jaxpr/ki,bim->bkm/dot_general | solution.py:29
  207.1 1.5 copy-done
  210.4 1.4 convolution_convert_fusion.8
  217.9 1.1 sine_convert_fusion.2
  219.4 2.7 %convolution_bitcast_fusion.5 = f32[4,512,512]{1,2,0:T(8,128)} fusion(bf16[4,256,512]{2,1,0:T(8,128)(2,1)S(1)} %bitcast.101, bf16[256,256]{1,0:T(8,128)(2,1)S(1)} %get-tuple-element.251, bf16[256,256]{1,0:T(8,128)(2,1)S(1)} %get-tuple-element.250), kind=kOutput, calls=%fused_computation.clone.1 | convolution fusion | flops 537395200 | bytes 5505024 | tf_op jit(solution)/shard_map/while/body/eval_jaxpr/ki,bim->bkm/dot_general | solution.py:29
  226.2 1.5 copy-done
  229.4 1.4 convolution_convert_fusion.8
  236.9 1.1 sine_convert_fusion.2
  238.5 2.7 %convolution_bitcast_fusion.5 = f32[4,512,512]{1,2,0:T(8,128)} fusion(bf16[4,256,512]{2,1,0:T(8,128)(2,1)S(1)} %bitcast.101, bf16[256,256]{1,0:T(8,128)(2,1)S(1)} %get-tuple-element.251, bf16[256,256]{1,0:T(8,128)(2,1)S(1)} %get-tuple-element.250), kind=kOutput, calls=%fused_computation.clone.1 | convolution fusion | flops 537395200 | bytes 5505024 | tf_op jit(solution)/shard_map/while/body/eval_jaxpr/ki,bim->bkm/dot_general | solution.py:29
  245.2 1.5 copy-done
  248.4 1.4 convolution_convert_fusion.8
  (423 shorter events, 74.9 us)
Async XLA Ops:
  1.9 55.6 %collective-permute-start.8 = (f32[256,512]{0,1:T(8,128)S(1)}, f32[256,512]{0,1:T(8,128)S(1)}, u32[]{:S(2)}, u32[]{:S(2)}) collective-permute-start(f32[256,512]{0,1:T(8,128)S(1)} %bitcast.108), channel_id=1, source_target_pairs={{16,0},{32,16},{48,32},{64,48},{80,64},{96,80},{112,96},{128,112},... | collective-permute-start | bytes 1572872 | tf_op jit(solution)/shard_map/ppermute | solution.py:18
  11.6 44.1 %collective-permute-start.1 = (f32[32,512]{1,0:T(8,128)S(1)}, f32[32,512]{1,0:T(8,128)S(1)}, u32[]{:S(2)}, u32[]{:S(2)}) collective-permute-start(f32[32,512]{1,0:T(8,128)S(1)} %get-tuple-element.170), channel_id=1, source_target_pairs={{0,4},{1,5},{2,6},{3,7},{4,8},{5,9},{6,10},{7,11},{8,12},{9,13},{1... | collective-permute-start | bytes 196616 | tf_op jit(solution)/shard_map/ppermute | solution.py:18
  14.8 10.3 %collective-permute-start.2 = (f32[32,32]{1,0:T(8,128)S(1)}, f32[32,32]{1,0:T(8,128)S(1)}, u32[]{:S(2)}, u32[]{:S(2)}) collective-permute-start(f32[32,32]{1,0:T(8,128)S(1)} %get-tuple-element.175), channel_id=1, source_target_pairs={{0,3},{1,4},{2,5},{3,6},{4,7},{5,8},{6,9},{7,10},{8,11},{9,12},{10... | collective-permute-start | bytes 12296 | tf_op jit(solution)/shard_map/ppermute | solution.py:18
  18.7 14.5 %collective-permute-start = (f32[32,32]{1,0:T(8,128)S(1)}, f32[32,32]{1,0:T(8,128)S(1)}, u32[]{:S(2)}, u32[]{:S(2)}) collective-permute-start(f32[32,32]{1,0:T(8,128)S(1)} %get-tuple-element.174), channel_id=1, source_target_pairs={{0,5},{1,6},{2,7},{3,8},{4,9},{5,10},{6,11},{7,12},{8,13},{9,14},{... | collective-permute-start | bytes 12296 | tf_op jit(solution)/shard_map/ppermute | solution.py:18
  20.6 35.3 %collective-permute-start.6 = (f32[32,512]{1,0:T(8,128)S(1)}, f32[32,512]{1,0:T(8,128)S(1)}, u32[]{:S(2)}, u32[]{:S(2)}) collective-permute-start(f32[32,512]{1,0:T(8,128)S(1)} %get-tuple-element.171), channel_id=1, source_target_pairs={{4,0},{5,1},{6,2},{7,3},{8,4},{9,5},{10,6},{11,7},{12,8},{13,9},{1... | collective-permute-start | bytes 196616 | tf_op jit(solution)/shard_map/ppermute | solution.py:18
  25.2 23.9 %collective-permute-start.4 = (f32[256,32]{0,1:T(8,128)S(1)}, f32[256,32]{0,1:T(8,128)S(1)}, u32[]{:S(2)}, u32[]{:S(2)}) collective-permute-start(f32[256,32]{0,1:T(8,128)S(1)} %get-tuple-element.173), channel_id=1, source_target_pairs={{1,0},{2,1},{3,2},{4,3},{5,4},{6,5},{7,6},{8,7},{9,8},{10,9},{11,1... | collective-permute-start | bytes 98312 | tf_op jit(solution)/shard_map/ppermute | solution.py:18
  33.2 7.4 %collective-permute-start.5 = (f32[32,32]{1,0:T(8,128)S(1)}, f32[32,32]{1,0:T(8,128)S(1)}, u32[]{:S(2)}, u32[]{:S(2)}) collective-permute-start(f32[32,32]{1,0:T(8,128)S(1)} %get-tuple-element.176), channel_id=1, source_target_pairs={{3,0},{4,1},{5,2},{6,3},{7,4},{8,5},{9,6},{10,7},{11,8},{12,9},{13... | collective-permute-start | bytes 12296 | tf_op jit(solution)/shard_map/ppermute | solution.py:18
  40.6 6.5 %collective-permute-start.7 = (f32[32,32]{1,0:T(8,128)S(1)}, f32[32,32]{1,0:T(8,128)S(1)}, u32[]{:S(2)}, u32[]{:S(2)}) collective-permute-start(f32[32,32]{1,0:T(8,128)S(1)} %get-tuple-element.177), channel_id=1, source_target_pairs={{5,0},{6,1},{7,2},{8,3},{9,4},{10,5},{11,6},{12,7},{13,8},{14,9},{... | collective-permute-start | bytes 12296 | tf_op jit(solution)/shard_map/ppermute | solution.py:18
  47.2 8.5 %collective-permute-start.3 = (f32[256,32]{0,1:T(8,128)S(1)}, f32[256,32]{0,1:T(8,128)S(1)}, u32[]{:S(2)}, u32[]{:S(2)}) collective-permute-start(f32[256,32]{0,1:T(8,128)S(1)} %get-tuple-element.172), channel_id=1, source_target_pairs={{0,1},{1,2},{2,3},{3,4},{4,5},{5,6},{6,7},{7,8},{8,9},{9,10},{10,1... | collective-permute-start | bytes 98312 | tf_op jit(solution)/shard_map/ppermute | solution.py:18
  57.7 41.1 %collective-permute-start.15 = (f32[96,512]{0,1:T(8,128)S(1)}, f32[96,512]{0,1:T(8,128)S(1)}, u32[]{:S(2)}, u32[]{:S(2)}) collective-permute-start(f32[96,512]{0,1:T(8,128)S(1)} %get-tuple-element.167), channel_id=1, source_target_pairs={{4,0},{5,1},{6,2},{7,3},{8,4},{9,5},{10,6},{11,7},{12,8},{13,9},{1... | collective-permute-start | bytes 589832 | tf_op jit(solution)/shard_map/ppermute | solution.py:18
  59.6 39.2 %collective-permute-start.10 = (f32[96,512]{0,1:T(8,128)S(1)}, f32[96,512]{0,1:T(8,128)S(1)}, u32[]{:S(2)}, u32[]{:S(2)}) collective-permute-start(f32[96,512]{0,1:T(8,128)S(1)} %get-tuple-element.166), channel_id=1, source_target_pairs={{0,4},{1,5},{2,6},{3,7},{4,8},{5,9},{6,10},{7,11},{8,12},{9,13},{1... | collective-permute-start | bytes 589832 | tf_op jit(solution)/shard_map/ppermute | solution.py:18
  63.6 9.0 %collective-permute-start.14 = (f32[96,96]{0,1:T(8,128)S(1)}, f32[96,96]{0,1:T(8,128)S(1)}, u32[]{:S(2)}, u32[]{:S(2)}) collective-permute-start(f32[96,96]{0,1:T(8,128)S(1)} %get-tuple-element.164), channel_id=1, source_target_pairs={{3,0},{4,1},{5,2},{6,3},{7,4},{8,5},{9,6},{10,7},{11,8},{12,9},{13... | collective-permute-start | bytes 110600 | tf_op jit(solution)/shard_map/ppermute | solution.py:18
  65.6 33.1 %collective-permute-start.13 = (f32[256,96]{0,1:T(8,128)S(1)}, f32[256,96]{0,1:T(8,128)S(1)}, u32[]{:S(2)}, u32[]{:S(2)}) collective-permute-start(f32[256,96]{0,1:T(8,128)S(1)} %get-tuple-element.169), channel_id=1, source_target_pairs={{1,0},{2,1},{3,2},{4,3},{5,4},{6,5},{7,6},{8,7},{9,8},{10,9},{11,1... | collective-permute-start | bytes 294920 | tf_op jit(solution)/shard_map/ppermute | solution.py:18
  70.7 27.9 %collective-permute-start.12 = (f32[256,96]{0,1:T(8,128)S(1)}, f32[256,96]{0,1:T(8,128)S(1)}, u32[]{:S(2)}, u32[]{:S(2)}) collective-permute-start(f32[256,96]{0,1:T(8,128)S(1)} %get-tuple-element.168), channel_id=1, source_target_pairs={{0,1},{1,2},{2,3},{3,4},{4,5},{5,6},{6,7},{7,8},{8,9},{9,10},{10,1... | collective-permute-start | bytes 294920 | tf_op jit(solution)/shard_map/ppermute | solution.py:18
  72.7 8.9 %collective-permute-start.11 = (f32[96,96]{0,1:T(8,128)S(1)}, f32[96,96]{0,1:T(8,128)S(1)}, u32[]{:S(2)}, u32[]{:S(2)}) collective-permute-start(f32[96,96]{0,1:T(8,128)S(1)} %get-tuple-element.165), channel_id=1, source_target_pairs={{0,3},{1,4},{2,5},{3,6},{4,7},{5,8},{6,9},{7,10},{8,11},{9,12},{10... | collective-permute-start | bytes 110600 | tf_op jit(solution)/shard_map/ppermute | solution.py:18
  81.6 10.2 %collective-permute-start.9 = (f32[96,96]{0,1:T(8,128)S(1)}, f32[96,96]{0,1:T(8,128)S(1)}, u32[]{:S(2)}, u32[]{:S(2)}) collective-permute-start(f32[96,96]{0,1:T(8,128)S(1)} %get-tuple-element.162), channel_id=1, source_target_pairs={{0,5},{1,6},{2,7},{3,8},{4,9},{5,10},{6,11},{7,12},{8,13},{9,14},{... | collective-permute-start | bytes 110600 | tf_op jit(solution)/shard_map/ppermute | solution.py:18
  91.8 6.9 %collective-permute-start.16 = (f32[96,96]{0,1:T(8,128)S(1)}, f32[96,96]{0,1:T(8,128)S(1)}, u32[]{:S(2)}, u32[]{:S(2)}) collective-permute-start(f32[96,96]{0,1:T(8,128)S(1)} %get-tuple-element.163), channel_id=1, source_target_pairs={{5,0},{6,1},{7,2},{8,3},{9,4},{10,5},{11,6},{12,7},{13,8},{14,9},{... | collective-permute-start | bytes 110600 | tf_op jit(solution)/shard_map/ppermute | solution.py:18
  110.3 0.9 copy-start.3
  111.2 0.8 copy-start.1
  111.2 0.8 copy-start.2
  111.2 2.2 copy-start
  116.6 0.8 copy-start.4
  116.6 0.9 copy-start.5
  129.3 0.9 copy-start.3
  130.2 0.8 copy-start.1
  130.2 0.8 copy-start.2
  130.3 2.2 copy-start
  135.6 0.8 copy-start.4
  135.6 0.9 copy-start.5
  148.3 0.9 copy-start.3
  149.3 0.8 copy-start.1
  149.3 0.8 copy-start.2
  149.3 2.2 copy-start
  154.6 0.8 copy-start.4
  154.6 0.9 copy-start.5
  167.4 0.9 copy-start.3
  168.3 0.8 copy-start.1
  168.3 0.8 copy-start.2
  168.3 2.2 copy-start
  173.7 0.8 copy-start.4
  173.7 0.9 copy-start.5
  186.4 0.9 copy-start.3
  187.3 0.8 copy-start.1
  187.3 0.8 copy-start.2
  187.3 2.2 copy-start
  192.7 0.8 copy-start.4
  192.7 0.9 copy-start.5
  205.4 0.9 copy-start.3
  206.4 0.8 copy-start.1
  206.4 0.8 copy-start.2
  206.4 2.2 copy-start
  211.7 0.8 copy-start.4
  211.7 0.9 copy-start.5
  224.5 0.9 copy-start.3
  225.4 0.8 copy-start.1
  225.4 2.2 copy-start
  230.8 0.8 copy-start.4
  230.8 0.9 copy-start.5
  243.5 0.9 copy-start.3
  244.4 0.8 copy-start.1
  244.4 0.8 copy-start.2
  244.5 2.2 copy-start
  249.8 0.8 copy-start.4
  249.8 0.9 copy-start.5
  (1 other events, 0.8 us)
where the time goes:
time: 255 us; the launch traced here: 253 us
  starting transfers between devices  59.8 us (23%)
  matrix products  47.1 us (18%)
  local copies, waits for them, and re-layouts  47 us (18%)
  other arithmetic  43.4 us (17%)
  waiting for transfers between devices  31.6 us (12%)
  loops' own time  22.8 us (9%)
    ppermute x17, starting transfers between devices, passed_along(): lax.ppermute(value, axis, [(source, source + steps) for source in range(l...  59.8 us
    ppermute x17, waiting for transfers between devices, passed_along(): lax.ppermute(value, axis, [(source, source + steps) for source in range(l...  31.6 us
    dot_general x24, matrix products, narrow_product(): jnp.einsum('ki,bim->bkm', left_matrix, operand, preferred_element_type=jn...  30.5 us
    another operation x1, loops' own time, local(): lax.map(one_group, jnp.arange(patch_rows * group_count, dtype=jnp.int32))  22.8 us
    while x112, local copies, waits for them, and re-layouts  17.8 us
    dot_general x8, matrix products, correlate(): returned = jnp.dot(joined, mixing, preferred_element_type=jnp.float32)  10.9 us
    convert_element_type x8, other arithmetic, spectral_tables(): jnp.sin(phase_angle).astype(jnp.bfloat16)  8.78 us
    dynamic_slice x8, local copies, waits for them, and re-layouts, one_group(): lax.dynamic_slice(own_ext, (band_row, column_start), (PATCH, 5 * stride))  8.63 us
  transfers between devices with their start and end apart: 17, of which 7 were waited for; matrix products, arithmetic and copies ran while one was open for 2% of the time, Pallas kernels for 0%

commit v1 on v0

v1 whole, which is shorter than its diff:
```python
import functools

import jax
import jax.numpy as jnp
import ml_dtypes
import numpy as np
from jax import lax
from jax.experimental import pallas as pl
from jax.experimental.pallas import tpu as pltpu
from jax.sharding import PartitionSpec as P

MESH = pl.DeviceIdType.MESH
F32 = jnp.float32
BF16 = jnp.bfloat16

PATCH = 128
WIN = 256
TH = 256
TW = 512
TCOLS = 4
TROWS = 4
SECS = 16
STRIDE = 64
WM = 96
PM = 32
LANE = 128
WROWS = TH + 2 * WM
PROWS = TH + 2 * PM
WIDE = TW + 2 * LANE
COUNT = 32


def table():
    b = np.arange(WIN)[:, None]
    turn = (b * (2 * np.arange(PATCH)[None, :] + 1)) % (2 * WIN)
    angle = turn * (np.pi / WIN)
    return np.concatenate([np.cos(angle), np.sin(angle)], 1).astype(np.float32).astype(ml_dtypes.bfloat16)


def standard(x):
    size = float(x.shape[0] * x.shape[1])
    centre = jnp.sum(x, keepdims=True) * (1.0 / size)
    deviation = x - centre
    spread = jnp.sum(deviation * deviation, keepdims=True) * (1.0 / size)
    return (deviation * lax.rsqrt(spread + 1e-5)).astype(BF16)


def dot(a, b):
    return jnp.dot(a, b, preferred_element_type=F32)


def four(z):
    p, r = z[:PATCH, :PATCH], z[:PATCH, PATCH:]
    t, q = z[PATCH:, :PATCH], z[PATCH:, PATCH:]
    return p - q, r + t, p + q, r - t


def window_spectrum(x, tc, tr):
    wa = dot(standard(x), tc).astype(BF16)
    return four(dot(tr, wa))


def patch_scores(x, g, tc, tr):
    pa = dot(standard(x), tc[:PATCH, :]).astype(BF16)
    f = [v.astype(BF16).astype(F32) for v in four(dot(tr[:, :PATCH], pa))]
    g = [v.astype(F32) for v in g]
    xr = f[0] * g[0] + f[1] * g[1]
    xi = f[1] * g[0] - f[0] * g[1]
    yr = f[2] * g[2] + f[3] * g[3]
    yi = f[3] * g[2] - f[2] * g[3]
    upper = jnp.concatenate([(xr + yr).astype(BF16), (-(xi + yi)).astype(BF16)], 1)
    lower = jnp.concatenate([(yi - xi).astype(BF16), (yr - xr).astype(BF16)], 1)
    back = dot(tc[:PATCH, :], jnp.concatenate([upper, lower], 0)).astype(BF16)
    return dot(back, tr[:, :PATCH]) * (1.0 / (32768.0 * 128.0))


def kernel(sec_ref, fol_ref, tc_ref, tr_ref, flow_ref, strength_ref,
           wx, px, fx, e_win, e_pat, spec, peak, res, res_in, lsem, wsend, wrecv, psend, precv, rsem):
    s, t = lax.axis_index("sec"), lax.axis_index("tile")
    r, c = t // TCOLS, lax.rem(t, TCOLS)
    after, before = lax.rem(s + 1, SECS), lax.rem(s + SECS - 1, SECS)
    has_up, has_down, has_left, has_right = r > 0, r < TROWS - 1, c > 0, c < TCOLS - 1
    up, down, left, right = (s, t - TCOLS), (s, t + TCOLS), (s, t - 1), (s, t + 1)
    first = s == 0
    sides = [(has_left, left), (has_right, right), (has_up, up), (has_down, down)]

    barrier = pltpu.get_barrier_semaphore()
    for d in ((after, t), (before, t)):
        pl.semaphore_signal(barrier, inc=1, device_id=d, device_id_type=MESH)
    for ok, d in sides:
        @pl.when(ok)
        def _():
            pl.semaphore_signal(barrier, inc=1, device_id=d, device_id_type=MESH)
    near = sum(ok.astype(jnp.int32) for ok, _ in sides)
    pl.semaphore_wait(barrier, 2 + near)

    def remote(src, dst, ssem, rsem, d):
        return pltpu.make_async_remote_copy(src_ref=src, dst_ref=dst, send_sem=ssem, recv_sem=rsem,
                                            device_id=d, device_id_type=MESH)

    own = sec_ref.at[0, 0]
    far = remote(own, px.at[pl.ds(PM, TH), pl.ds(LANE, TW)], psend.at[0], precv.at[0], (after, t))
    far.start()

    edge = TW - LANE
    wcols = [
        (has_left, has_right, remote(own.at[:, pl.ds(0, LANE)], wx.at[pl.ds(WM, TH), pl.ds(LANE + TW, LANE)], wsend.at[0], wrecv.at[0], left)),
        (has_right, has_left, remote(own.at[:, pl.ds(edge, LANE)], wx.at[pl.ds(WM, TH), pl.ds(0, LANE)], wsend.at[1], wrecv.at[1], right)),
    ]
    wrows = [
        (has_up, has_down, remote(own.at[pl.ds(0, WM)], wx.at[pl.ds(WM + TH, WM), pl.ds(LANE, TW)], wsend.at[2], wrecv.at[2], up)),
        (has_down, has_up, remote(own.at[pl.ds(TH - WM, WM)], wx.at[pl.ds(0, WM), pl.ds(LANE, TW)], wsend.at[3], wrecv.at[3], down)),
    ]

    def corners(buf, m, ssem, rsem, base):
        out = []
        for i, (side, lane) in enumerate(((has_left, 0), (has_right, LANE + TW))):
            lanes = pl.ds(lane, LANE)
            out.append((side & has_up, side & has_down, remote(
                buf.at[pl.ds(m, m), lanes], buf.at[pl.ds(m + TH, m), lanes], ssem.at[base + 2 * i], rsem.at[base + 2 * i], up)))
            out.append((side & has_down, side & has_up, remote(
                buf.at[pl.ds(TH, m), lanes], buf.at[pl.ds(0, m), lanes], ssem.at[base + 2 * i + 1], rsem.at[base + 2 * i + 1], down)))
        return out

    wcorners = corners(wx, WM, wsend, wrecv, 4)

    def start(copies):
        for ok, _, copy in copies:
            @pl.when(ok)
            def _():
                copy.start()

    def wait_recv(copies):
        for _, ok, copy in copies:
            @pl.when(ok)
            def _():
                copy.wait_recv()

    def wait_send(copies):
        for ok, _, copy in copies:
            @pl.when(ok)
            def _():
                copy.wait_send()

    @pl.when(jnp.logical_not(first))
    def _():
        start(wcols)
        start(wrows)

    centre = pltpu.make_async_copy(own, wx.at[pl.ds(WM, TH), pl.ds(LANE, TW)], lsem.at[0])
    spare = pltpu.make_async_copy(fol_ref.at[0], fx, lsem.at[0])

    @pl.when(jnp.logical_not(first))
    def _():
        centre.start()

    @pl.when(first)
    def _():
        spare.start()

    for buf, m in ((wx, WM), (px, PM)):
        rows = TH + 2 * m

        @pl.when(jnp.logical_not(has_up))
        def _():
            buf[0:m, :] = jnp.zeros((m, WIDE), F32)

        @pl.when(jnp.logical_not(has_down))
        def _():
            buf[m + TH:, :] = jnp.zeros((m, WIDE), F32)

        @pl.when(jnp.logical_not(has_left))
        def _():
            buf[:, 0:LANE] = jnp.zeros((rows, LANE), F32)

        @pl.when(jnp.logical_not(has_right))
        def _():
            buf[:, LANE + TW:] = jnp.zeros((rows, LANE), F32)

    @pl.when(jnp.logical_not(first))
    def _():
        wait_recv(wcols)
        start(wcorners)
        wait_recv(wrows)
        wait_recv(wcorners)
        centre.wait()
        for k in range(2):
            lane = LANE - WM + STRIDE * k
            e_win[k] = wx[:, lane:lane + 640]
        wait_send(wcols)
        wait_send(wrows)
        wait_send(wcorners)

    @pl.when(first)
    def _():
        spare.wait()
        for k in range(2):
            e_win[k] = fx[:, STRIDE * k:STRIDE * k + 640]

    tc, tr = tc_ref[...], tr_ref[...]

    def window_step(n, carry):
        i, j = n // 4, lax.rem(n, 4)
        rows = pl.ds(pl.multiple_of(i * STRIDE, STRIDE), WIN)
        lanes = pl.ds(pl.multiple_of(j * LANE, LANE), WIN)
        for k in range(2):
            for m, g in enumerate(window_spectrum(e_win[k, rows, lanes], tc, tr)):
                spec[n, k, m] = g.astype(BF16)
        return carry

    lax.fori_loop(0, 16, window_step, 0)

    far.wait_recv()
    pcols = [
        (has_left, has_right, remote(px.at[pl.ds(PM, TH), pl.ds(LANE, LANE)], px.at[pl.ds(PM, TH), pl.ds(LANE + TW, LANE)], psend.at[1], precv.at[1], left)),
        (has_right, has_left, remote(px.at[pl.ds(PM, TH), pl.ds(TW, LANE)], px.at[pl.ds(PM, TH), pl.ds(0, LANE)], psend.at[2], precv.at[2], right)),
    ]
    prows = [
        (has_up, has_down, remote(px.at[pl.ds(PM, PM), pl.ds(LANE, TW)], px.at[pl.ds(PM + TH, PM), pl.ds(LANE, TW)], psend.at[3], precv.at[3], up)),
        (has_down, has_up, remote(px.at[pl.ds(TH, PM), pl.ds(LANE, TW)], px.at[pl.ds(0, PM), pl.ds(LANE, TW)], psend.at[4], precv.at[4], down)),
    ]
    pcorners = corners(px, PM, psend, precv, 5)
    start(pcols)
    start(prows)
    wait_recv(pcols)
    start(pcorners)
    wait_recv(prows)
    wait_recv(pcorners)
    for k in range(2):
        lane = LANE - PM + STRIDE * k
        e_pat[k] = px[:, lane:lane + TW]

    offset = lax.broadcasted_iota(jnp.int32, (PATCH // 8, 8, PATCH), 0) * 8 + lax.broadcasted_iota(jnp.int32, (PATCH // 8, 8, PATCH), 1)
    offset = (offset - PATCH // 2).astype(F32)

    def patch_step(n, carry):
        i, j = n // 4, lax.rem(n, 4)
        rows = pl.ds(pl.multiple_of(i * STRIDE, STRIDE), PATCH)
        lanes = pl.ds(pl.multiple_of(j * LANE, LANE), PATCH)
        for k in range(2):
            score = patch_scores(e_pat[k, rows, lanes], [spec[n, k, m] for m in range(4)], tc, tr)
            score = score.reshape(PATCH // 8, 8, PATCH)
            high = jnp.max(score, axis=0)
            weight = jnp.exp(score - high[None])
            peak[0, 2 * n + k] = high
            peak[1, 2 * n + k] = jnp.sum(weight, axis=0)
            peak[2, 2 * n + k] = jnp.sum(weight * offset, axis=0)
        return carry

    lax.fori_loop(0, 16, patch_step, 0)

    high = peak[0]
    top = jnp.max(jnp.max(high, axis=1, keepdims=True), axis=2, keepdims=True)
    scale = jnp.exp(high - top)
    weight = peak[1] * scale
    column = (lax.broadcasted_iota(jnp.int32, (COUNT, 8, LANE), 2) - PATCH // 2).astype(F32)

    def total(x):
        return jnp.sum(jnp.sum(x, axis=1, keepdims=True), axis=2, keepdims=True)

    whole = total(weight)
    by_row = total(peak[2] * scale) / whole
    by_col = total(weight * column) / whole
    strength = (top + jnp.log(whole)) * (1.0 / 128.0)
    place = lax.broadcasted_iota(jnp.int32, (COUNT, 1, LANE), 0) == lax.broadcasted_iota(jnp.int32, (COUNT, 1, LANE), 2)
    for k, v in enumerate((by_row, by_col, strength)):
        res[k:k + 1, :] = jnp.sum(jnp.where(place, v, 0.0), axis=0)

    back = remote(res, res_in, rsem.at[0], rsem.at[1], (before, t))
    back.start()
    far.wait_send()
    wait_send(pcols)
    wait_send(prows)
    wait_send(pcorners)
    back.wait()
    flow_ref[0, 0] = res_in[0:2, 0:COUNT]
    strength_ref[0] = res_in[2:3, 0:COUNT]


def solution(mesh):
    tc = table()

    def local(sections, following):
        dma = pltpu.SemaphoreType.DMA
        return pl.pallas_call(
            kernel,
            out_shape=(jax.ShapeDtypeStruct((1, 1, 2, COUNT), F32), jax.ShapeDtypeStruct((1, 1, COUNT), F32)),
            in_specs=[pl.BlockSpec(memory_space=pl.ANY)] * 2 + [pl.BlockSpec(memory_space=pltpu.VMEM)] * 2,
            out_specs=(pl.BlockSpec(memory_space=pltpu.VMEM),) * 2,
            scratch_shapes=[
                pltpu.VMEM((WROWS, WIDE), F32),
                pltpu.VMEM((PROWS, WIDE), F32),
                pltpu.VMEM((WROWS, TW + 2 * WM), F32),
                pltpu.VMEM((2, WROWS, 640), F32),
                pltpu.VMEM((2, PROWS, TW), F32),
                pltpu.VMEM((16, 2, 4, PATCH, PATCH), BF16),
                pltpu.VMEM((3, COUNT, 8, LANE), F32),
                pltpu.VMEM((8, LANE), F32),
                pltpu.VMEM((8, LANE), F32),
                dma((1,)), dma((8,)), dma((8,)), dma((9,)), dma((9,)), dma((2,)),
            ],
            compiler_params=pltpu.CompilerParams(collective_id=0, has_side_effects=True, vmem_limit_bytes=40 * 2**20),
            name="patch_flow",
        )(sections, following, jnp.asarray(tc), jnp.asarray(np.ascontiguousarray(tc.T)))

    return jax.shard_map(
        local,
        mesh=mesh,
        in_specs=(P("sec", "tile", None, None), P("tile", None, None)),
        out_specs=(P("sec", "tile", None, None), P("sec", "tile", None)),
        check_vma=False,
    )
```

time: 255 us -> 83.2 us (0.33)
  the two profiles are of different devices: /device:TPU:22 before, /device:TPU:1 now
where the time goes in v1:
time: 83.2 us; the launch traced here: 83 us
  Pallas kernels  77.1 us (93%)
  local copies, waits for them, and re-layouts  5.26 us (6%)
    pallas_call x1, Pallas kernels, local(): pl.pallas_call(kernel, out_shape=(jax.ShapeDtypeStruct((1, 1, 2, COUNT),...  77.1 us
    unnamed x10, local copies, waits for them, and re-layouts  5.26 us

profile of v1, /device:TPU:1, one launch (start us, length us, event | category | flops | bytes accessed | tf_op | source)
XLA Modules:
  0.0 83.0 jit_solution(8180818623684469988)
XLA Ops:
  0.6 0.0 copy-start
  0.6 1.3 %copy-done = f32[1,448,704]{2,1,0:T(8,128)S(1)} copy-done((f32[1,448,704]{2,1,0:T(8,128)S(1)}, f32[1,448,704]{2,1,0:T(8,128)}, u32[]{:S(2)}) %copy-start) | copy-done | bytes 1261592
  2.0 0.0 copy-start.1
  2.0 1.0 %copy-done.1 = f32[1,1,256,512]{3,2,1,0:T(8,128)S(1)} copy-done((f32[1,1,256,512]{3,2,1,0:T(8,128)S(1)}, f32[1,1,256,512]{3,2,1,0:T(8,128)}, u32[]{:S(2)}) %copy-start.1) | copy-done | bytes 524312
  3.0 0.0 copy-start.2
  3.0 0.9 %copy-done.2 = bf16[256,256]{1,0:T(8,128)(2,1)S(1)} copy-done((bf16[256,256]{1,0:T(8,128)(2,1)S(1)}, bf16[256,256]{1,0:T(8,128)(2,1)}, u32[]{:S(2)}) %copy-start.2) | copy-done | bytes 131096
  3.9 0.0 copy-start.3
  3.9 0.9 %copy-done.3 = bf16[256,256]{1,0:T(8,128)(2,1)S(1)} copy-done((bf16[256,256]{1,0:T(8,128)(2,1)S(1)}, bf16[256,256]{1,0:T(8,128)(2,1)}, u32[]{:S(2)}) %copy-start.3) | copy-done | bytes 131096
  4.8 77.1 %patch_flow.1 = (f32[1,1,2,32]{3,2,1,0:T(2,128)S(1)}, f32[1,1,32]{2,1,0:T(1,128)S(1)}) custom-call(f32[1,1,256,512]{3,2,1,0:T(8,128)S(1)} %copy-done.1, f32[1,448,704]{2,1,0:T(8,128)S(1)} %copy-done, bf16[256,256]{1,0:T(8,128)(2,1)S(1)} %copy-done.3, bf16[256,256]{1,0:T(8,128)(2,1)S(1)} %copy-done.2), custom_call_target="tpu_custom_call" | custom-call | tf_op jit(solution)/shard_map/patch_flow/pallas_call | solution.py:285
  82.0 0.6 copy.8
  82.5 0.5 copy.9
Async XLA Ops:
  0.6 1.3 %copy-start = (f32[1,448,704]{2,1,0:T(8,128)S(1)}, f32[1,448,704]{2,1,0:T(8,128)}, u32[]{:S(2)}) copy-start(f32[1,448,704]{2,1,0:T(8,128)} %fol_ref.1) | copy-start | bytes 3784708
  2.0 1.0 %copy-start.1 = (f32[1,1,256,512]{3,2,1,0:T(8,128)S(1)}, f32[1,1,256,512]{3,2,1,0:T(8,128)}, u32[]{:S(2)}) copy-start(f32[1,1,256,512]{3,2,1,0:T(8,128)} %sec_ref.1) | copy-start | bytes 1572868
  3.0 0.9 %copy-start.2 = (bf16[256,256]{1,0:T(8,128)(2,1)S(1)}, bf16[256,256]{1,0:T(8,128)(2,1)}, u32[]{:S(2)}) copy-start(bf16[256,256]{1,0:T(8,128)(2,1)} %constant.5.clone.tr_ref) | copy-start | bytes 393220
  3.9 0.9 %copy-start.3 = (bf16[256,256]{1,0:T(8,128)(2,1)S(1)}, bf16[256,256]{1,0:T(8,128)(2,1)}, u32[]{:S(2)}) copy-start(bf16[256,256]{1,0:T(8,128)(2,1)} %constant.4.clone.tc_ref) | copy-start | bytes 393220

commit v2 on v1

v2 whole, which is shorter than its diff:
```python
import jax
import jax.numpy as jnp
import ml_dtypes
import numpy as np
from jax import lax
from jax.experimental import pallas as pl
from jax.experimental.pallas import tpu as pltpu
from jax.sharding import PartitionSpec as P

MESH = pl.DeviceIdType.MESH
F32 = jnp.float32
BF16 = jnp.bfloat16

PATCH = 128
WIN = 256
TH = 256
TW = 512
TCOLS = 4
TROWS = 4
SECS = 16
STRIDE = 64
WM = 96
PM = 32
LANE = 128
WROWS = TH + 2 * WM
PROWS = TH + 2 * PM
WIDE = TW + 2 * LANE
SPAN = TW + 2 * WM
COUNT = 32
CUTS = 4


def tables():
    b = np.arange(WIN)[:, None]
    turn = (b * (2 * np.arange(PATCH)[None, :] + 1)) % (2 * WIN)
    angle = turn * (np.pi / WIN)
    tc = np.concatenate([np.cos(angle), np.sin(angle)], 1)
    cr, sr = tc[:PATCH, :PATCH].T, tc[:PATCH, PATCH:].T
    four = np.concatenate([np.concatenate(x, 1) for x in ((cr, -sr), (sr, cr), (cr, sr), (-sr, cr))], 0)
    return [np.ascontiguousarray(v).astype(np.float32).astype(ml_dtypes.bfloat16) for v in (tc, tc.T, four)]


def dot(a, b):
    return jnp.dot(a, b, preferred_element_type=F32)


def tree(x):
    rows = x.shape[0]
    while rows > 8:
        rows //= 2
        x = x[:rows] + x[rows:]
    for h in (4, 2, 1):
        x = x + pltpu.roll(x, h, 0)
    return x


def strip_moments(x):
    mean = tree(x) * (1.0 / STRIDE)
    dev = x.reshape(STRIDE // 8, 8, x.shape[1]) - mean[None]
    return mean, tree((dev * dev).reshape(x.shape))


def merge(mean, dev2, size, shift, axis):
    n = mean.shape[axis]
    other = pltpu.roll(mean, n - shift, axis)
    gap = mean - other
    return (mean + other) * 0.5, dev2 + pltpu.roll(dev2, n - shift, axis) + gap * gap * (0.5 * size), 2 * size


def moments(strips, extent):
    sub = lax.broadcasted_iota(jnp.int32, (8, strips[0].shape[1]), 0)
    mean = jnp.zeros(sub.shape, F32)
    dev2 = jnp.zeros(sub.shape, F32)
    for i, x in enumerate(strips):
        m, d = strip_moments(x)
        mean = jnp.where(sub == i, m, mean)
        dev2 = jnp.where(sub == i, d, dev2)
    size = float(STRIDE)
    h = 1
    while h < extent:
        mean, dev2, size = merge(mean, dev2, size, h, 1)
        h *= 2
    h = STRIDE
    while h < extent:
        mean, dev2, size = merge(mean, dev2, size, h // STRIDE, 0)
        h *= 2
    return mean, lax.rsqrt(dev2 * (1.0 / size) + 1e-5)


def spread_out(stat, out, base, rows=8):
    for j in range(8):
        lane = base + STRIDE * j
        out[j, 0:rows] = jnp.broadcast_to(stat[:rows, lane:lane + 1], (rows, LANE))


def window_row(i, e0, e1, cen, tc, tr, spec):
    rows = pl.ds(pl.multiple_of(i * STRIDE, STRIDE), WIN)
    for j in range(8):
        e = (e0, e1)[j % 2]
        x = (e[rows, pl.ds(LANE * (j // 2), WIN)] - cen[j, pl.ds(i, 1), 0:1]).astype(BF16)
        z = dot(tr[...], dot(x, tc[...]).astype(BF16))
        p, r = z[:PATCH, :PATCH], z[:PATCH, PATCH:]
        t, q = z[PATCH:, :PATCH], z[PATCH:, PATCH:]
        for m, g in enumerate((p - q, r + t, p + q, r - t)):
            spec[i * 4 + j // 2, m, :, pl.ds(LANE * (j % 2), LANE)] = g.astype(BF16)


def cross(f, g):
    f = [v.astype(F32) for v in f]
    g = [v.astype(F32) for v in g]
    xr = f[0] * g[0] + f[1] * g[1]
    xi = f[0] * g[1] - f[1] * g[0]
    yr = f[2] * g[2] + f[3] * g[3]
    yi = f[2] * g[3] - f[3] * g[2]
    return [v.astype(BF16) for v in (xr + yr, xi + yi, xi - yi, yr - xr)]


def patch_row(i, px, pcen, pinv, winv, tc, tr, t4, spec, peak):
    rows = pl.ds(STRIDE * i, PATCH)
    offset = lax.broadcasted_iota(jnp.int32, (PATCH // 8, 8, PATCH), 0) * 8
    offset = offset + lax.broadcasted_iota(jnp.int32, (PATCH // 8, 8, PATCH), 1)
    offset = (offset - PATCH // 2).astype(F32)
    band = px[rows, :]
    x = []
    for j in range(8):
        lane = LANE - PM + STRIDE * j
        x.append((band[:, lane:lane + PATCH] - pcen[j, i:i + 1, 0:1]).astype(BF16))
    a = dot(jnp.concatenate(x, 0), tc[:PATCH, :]).astype(BF16)
    fs = []
    for jj in range(4):
        e, o = a[256 * jj:256 * jj + 128], a[256 * jj + 128:256 * jj + 256]
        upper = jnp.concatenate([e[:, :LANE], o[:, :LANE]], 1)
        lower = jnp.concatenate([e[:, LANE:], o[:, LANE:]], 1)
        fs.append(dot(t4[...], jnp.concatenate([upper, lower], 0)).astype(BF16))
    lhs = []
    for jj in range(4):
        f = [fs[jj][LANE * m:LANE * m + LANE] for m in range(4)]
        ar, ai, di, dr = cross(f, [spec[i * 4 + jj, m] for m in range(4)])
        for k in range(2):
            h = slice(LANE * k, LANE * k + LANE)
            lhs += [jnp.concatenate([ar[:, h], ai[:, h]], 1), jnp.concatenate([di[:, h], dr[:, h]], 1)]
    uv = dot(jnp.concatenate(lhs, 0), tr[:, :PATCH]).astype(BF16)
    for jj in range(4):
        s = dot(tc[:PATCH, :], jnp.concatenate([uv[512 * jj:512 * jj + 256], uv[512 * jj + 256:512 * jj + 512]], 1))
        for k in range(2):
            j = 2 * jj + k
            scale = pinv[j, i:i + 1, :] * winv[j, i:i + 1, :] * (1.0 / (32768.0 * 128.0))
            score = (s[:, LANE * k:LANE * k + LANE] * scale).reshape(PATCH // 8, 8, PATCH)
            high = jnp.max(score, axis=0)
            weight = jnp.exp(score - high[None])
            peak[0, i * 8 + j] = high
            peak[1, i * 8 + j] = jnp.sum(weight, axis=0)
            peak[2, i * 8 + j] = jnp.sum(weight * offset, axis=0)


def finish(peak, res):
    high = peak[0]
    top = jnp.max(jnp.max(high, axis=1, keepdims=True), axis=2, keepdims=True)
    scale = jnp.exp(high - top)
    weight = peak[1] * scale
    column = (lax.broadcasted_iota(jnp.int32, (COUNT, 8, LANE), 2) - PATCH // 2).astype(F32)

    def total(x):
        return jnp.sum(jnp.sum(x, axis=1, keepdims=True), axis=2, keepdims=True)

    whole = total(weight)
    by_row = total(peak[2] * scale) / whole
    by_col = total(weight * column) / whole
    strength = (top + jnp.log(whole)) * (1.0 / 128.0)
    place = lax.broadcasted_iota(jnp.int32, (COUNT, 1, LANE), 0) == lax.broadcasted_iota(jnp.int32, (COUNT, 1, LANE), 2)
    for k, v in enumerate((by_row, by_col, strength)):
        res[k:k + 1, :] = jnp.sum(jnp.where(place, v, 0.0), axis=0)


def pack(x, lane):
    group = lax.broadcasted_iota(jnp.int32, (16, LANE), 1) // PM
    out = jnp.zeros((16, LANE), F32)
    for g in range(4):
        part = x[16 * g:16 * g + 16]
        shift = (PM * g - lane) % LANE
        out = jnp.where(group == g, pltpu.roll(part, shift, 1) if shift else part, out)
    return out


def unpack(y, lane):
    out = []
    for g in range(4):
        shift = (lane - PM * g) % LANE
        out.append(pltpu.roll(y, shift, 1) if shift else y)
    return jnp.concatenate(out, 0)


def when(ok):
    return pl.when(ok)


def kernel(sec_ref, fol_ref, tc_ref, tr_ref, t4_ref, flow_ref, strength_ref,
           tc, tr, t4, wx, px, e0, e1, wcen, winv, pcen, pinv, spec, peak, out_cols, in_cols, res, res_in,
           lsem, wsend, wrecv, fsend, frecv, psend, precv, csend, crecv, rsem):
    s, t = lax.axis_index("sec"), lax.axis_index("tile")
    r, c = t // TCOLS, lax.rem(t, TCOLS)
    after, before = lax.rem(s + 1, SECS), lax.rem(s + SECS - 1, SECS)
    has_up, has_down, has_left, has_right = r > 0, r < TROWS - 1, c > 0, c < TCOLS - 1
    up, down, left, right = (s, t - TCOLS), (s, t + TCOLS), (s, t - 1), (s, t + 1)
    first = s == 0
    inner = jnp.logical_not(first)
    sides = [(has_left, left), (has_right, right), (has_up, up), (has_down, down)]

    barrier = pltpu.get_barrier_semaphore()
    for d in ((after, t), (before, t)):
        pl.semaphore_signal(barrier, inc=1, device_id=d, device_id_type=MESH)
    for ok, d in sides:
        @when(ok)
        def _():
            pl.semaphore_signal(barrier, inc=1, device_id=d, device_id_type=MESH)

    own = sec_ref.at[0, 0]
    constants = [pltpu.make_async_copy(a, b, lsem.at[1 + n]) for n, (a, b) in enumerate(((tc_ref, tc), (tr_ref, tr), (t4_ref, t4)))]
    centre = pltpu.make_async_copy(own, wx.at[pl.ds(WM, TH), pl.ds(LANE, TW)], lsem.at[0])
    spare = pltpu.make_async_copy(fol_ref.at[0], e0, lsem.at[0])

    @when(inner)
    def _():
        centre.start()

    @when(first)
    def _():
        spare.start()

    for copy in constants:
        copy.start()

    for buf, m in ((wx, WM), (px, PM)):
        rows = TH + 2 * m

        @when(jnp.logical_not(has_up))
        def _():
            buf[0:m, :] = jnp.zeros((m, WIDE), F32)

        @when(jnp.logical_not(has_down))
        def _():
            buf[m + TH:, :] = jnp.zeros((m, WIDE), F32)

        @when(jnp.logical_not(has_left))
        def _():
            buf[:, 0:LANE] = jnp.zeros((rows, LANE), F32)

        @when(jnp.logical_not(has_right))
        def _():
            buf[:, LANE + TW:] = jnp.zeros((rows, LANE), F32)

    res[...] = jnp.zeros((8, LANE), F32)

    near = sum(ok.astype(jnp.int32) for ok, _ in sides)
    pl.semaphore_wait(barrier, 2 + near)

    def remote(src, dst, ssem, rsem, d):
        return pltpu.make_async_remote_copy(src_ref=src, dst_ref=dst, send_sem=ssem, recv_sem=rsem,
                                            device_id=d, device_id_type=MESH)

    def start(copies):
        for ok, _, copy in copies:
            @when(ok)
            def _():
                copy.start()

    def wait_recv(copies):
        for _, ok, copy in copies:
            @when(ok)
            def _():
                copy.wait_recv()

    def wait_send(copies):
        for ok, _, copy in copies:
            @when(ok)
            def _():
                copy.wait_send()

    edge = TW - LANE
    wcols = [
        (has_left, has_right, remote(own.at[:, pl.ds(0, LANE)], wx.at[pl.ds(WM, TH), pl.ds(LANE + TW, LANE)], wsend.at[0], wrecv.at[0], left)),
        (has_right, has_left, remote(own.at[:, pl.ds(edge, LANE)], wx.at[pl.ds(WM, TH), pl.ds(0, LANE)], wsend.at[1], wrecv.at[1], right)),
    ]
    wrows = [
        (has_up, has_down, remote(own.at[pl.ds(0, WM)], wx.at[pl.ds(WM + TH, WM), pl.ds(LANE, TW)], wsend.at[2], wrecv.at[2], up)),
        (has_down, has_up, remote(own.at[pl.ds(TH - WM, WM)], wx.at[pl.ds(0, WM), pl.ds(LANE, TW)], wsend.at[3], wrecv.at[3], down)),
    ]

    def corners(buf, m, ssem, rsem, base):
        out = []
        for i, (side, lane) in enumerate(((has_left, 0), (has_right, LANE + TW))):
            lanes = pl.ds(lane, LANE)
            out.append((side & has_up, side & has_down, remote(
                buf.at[pl.ds(m, m), lanes], buf.at[pl.ds(m + TH, m), lanes], ssem.at[base + 2 * i], rsem.at[base + 2 * i], up)))
            out.append((side & has_down, side & has_up, remote(
                buf.at[pl.ds(TH, m), lanes], buf.at[pl.ds(0, m), lanes], ssem.at[base + 2 * i + 1], rsem.at[base + 2 * i + 1], down)))
        return out

    wcorners = corners(wx, WM, wsend, wrecv, 4)

    ranges = [(0, PM), (TH - PM, PM)] + [(PM + STRIDE * n, STRIDE) for n in range(CUTS - 1)]
    far = [remote(own.at[pl.ds(a, n)], px.at[pl.ds(PM + a, n), pl.ds(LANE, TW)], fsend.at[k], frecv.at[k], (after, t))
           for k, (a, n) in enumerate(ranges)]

    @when(inner)
    def _():
        start(wcols)
        start(wrows)

    for copy in far:
        copy.start()

    prows = [
        (has_up, has_down, remote(px.at[pl.ds(PM, PM), pl.ds(LANE, TW)], px.at[pl.ds(PM + TH, PM), pl.ds(LANE, TW)], psend.at[0], precv.at[0], up)),
        (has_down, has_up, remote(px.at[pl.ds(TH, PM), pl.ds(LANE, TW)], px.at[pl.ds(0, PM), pl.ds(LANE, TW)], psend.at[1], precv.at[1], down)),
    ]
    pcorners = corners(px, PM, psend, precv, 2)
    pcols = [[
        (has_left, has_right, remote(out_cols.at[2 * n], in_cols.at[2 * n], csend.at[2 * n], crecv.at[2 * n], left)),
        (has_right, has_left, remote(out_cols.at[2 * n + 1], in_cols.at[2 * n + 1], csend.at[2 * n + 1], crecv.at[2 * n + 1], right)),
    ] for n in range(CUTS)]

    def part(n):
        if n == 0:
            return [(PM, PM), (TH, PM)]
        return [(STRIDE * n, STRIDE)]

    def send_cols(n):
        for side, (ok, lane, at) in enumerate(((has_left, LANE, 0), (has_right, TW, LANE - PM))):
            @when(ok)
            def _():
                x = jnp.concatenate([px[a:a + m, lane:lane + LANE] for a, m in part(n)], 0)
                out_cols[2 * n + side] = pack(x, at)
        start(pcols[n])

    def take_cols(n):
        wait_recv(pcols[n])
        for side, (ok, lane, at) in enumerate(((has_right, LANE + TW, 0), (has_left, 0, LANE - PM))):
            @when(ok)
            def _():
                y = unpack(in_cols[2 * n + side], at)
                b = 0
                for a, m in part(n):
                    px[a:a + m, lane:lane + LANE] = y[b:b + m]
                    b += m

    @when(inner)
    def _():
        wait_recv(wcols)
        start(wcorners)

    for k in range(2):
        far[k].wait_recv()
    start(prows)
    send_cols(0)

    @when(inner)
    def _():
        wait_recv(wrows)
        wait_recv(wcorners)
        centre.wait()
        e0[...] = wx[:, LANE - WM:LANE - WM + SPAN]

    @when(first)
    def _():
        spare.wait()

    e1[...] = e0[:, STRIDE:]
    mean, inverse = moments(
        [jnp.concatenate([e0[STRIDE * i:STRIDE * i + STRIDE, :], jnp.zeros((STRIDE, WIDE - SPAN), F32)], 1) for i in range(7)], WIN)
    spread_out(mean, wcen, 0)
    spread_out(inverse, winv, 0)

    take_cols(0)
    start(pcorners)
    for copy in constants:
        copy.wait()

    def window_step(i, carry):
        window_row(i, e0, e1, wcen, tc, tr, spec)
        return carry

    lax.fori_loop(0, 4, window_step, 0)

    for n in range(1, CUTS):
        far[n + 1].wait_recv()
        send_cols(n)
        if n > 1:
            take_cols(n - 1)
    wait_recv(prows)
    wait_recv(pcorners)
    take_cols(CUTS - 1)
    mean, inverse = moments([px[STRIDE * i:STRIDE * i + STRIDE, :] for i in range(5)], PATCH)
    spread_out(mean, pcen, LANE - PM)
    spread_out(inverse, pinv, LANE - PM)
    for i in range(4):
        patch_row(i, px, pcen, pinv, winv, tc, tr, t4, spec, peak)
    finish(peak, res)
    back = remote(res, res_in, rsem.at[0], rsem.at[1], (before, t))
    back.start()

    @when(inner)
    def _():
        wait_send(wcols)
        wait_send(wrows)
        wait_send(wcorners)

    for copy in far:
        copy.wait_send()
    wait_send(prows)
    wait_send(pcorners)
    for copies in pcols:
        wait_send(copies)
    back.wait()
    flow_ref[0, 0] = res_in[0:2, 0:COUNT]
    strength_ref[0] = res_in[2:3, 0:COUNT]


def solution(mesh):
    tabs = tables()

    def local(sections, following):
        dma = pltpu.SemaphoreType.DMA
        vmem = pltpu.VMEM
        return pl.pallas_call(
            kernel,
            out_shape=(jax.ShapeDtypeStruct((1, 1, 2, COUNT), F32), jax.ShapeDtypeStruct((1, 1, COUNT), F32)),
            in_specs=[pl.BlockSpec(memory_space=pl.ANY)] * 5,
            out_specs=(pl.BlockSpec(memory_space=vmem),) * 2,
            scratch_shapes=[
                vmem((WIN, WIN), BF16), vmem((WIN, WIN), BF16), vmem((2 * WIN, WIN), BF16),
                vmem((WROWS, WIDE), F32),
                vmem((PROWS, WIDE), F32),
                vmem((WROWS, SPAN), F32),
                vmem((WROWS, SPAN - STRIDE), F32),
                vmem((8, 8, LANE), F32), vmem((8, 8, LANE), F32), vmem((8, 8, LANE), F32), vmem((8, 8, LANE), F32),
                vmem((16, 4, PATCH, WIN), BF16),
                vmem((3, COUNT, 8, LANE), F32),
                vmem((2 * CUTS, 16, LANE), F32),
                vmem((2 * CUTS, 16, LANE), F32),
                vmem((8, LANE), F32),
                vmem((8, LANE), F32),
                dma((4,)), dma((8,)), dma((8,)), dma((CUTS + 1,)), dma((CUTS + 1,)),
                dma((6,)), dma((6,)), dma((2 * CUTS,)), dma((2 * CUTS,)), dma((2,)),
            ],
            compiler_params=pltpu.CompilerParams(collective_id=0, has_side_effects=True, vmem_limit_bytes=58 * 2**20),
            name="patch_flow",
        )(sections, following, *[jnp.asarray(v) for v in tabs])

    return jax.shard_map(
        local,
        mesh=mesh,
        in_specs=(P("sec", "tile", None, None), P("tile", None, None)),
        out_specs=(P("sec", "tile", None, None), P("sec", "tile", None)),
        check_vma=False,
    )
```

time: 83.2 us -> 48.1 us (0.58)
  Pallas kernels: 77.1 us -> 44.1 us
  local copies, waits for them, and re-layouts: 5.26 us -> 2.36 us
    pallas_call x1, Pallas kernels: 77.1 us -> 44.1 us  [local(): pl.pallas_call(kernel, out_shape=(jax.ShapeDtypeStruct((1, 1, 2, COUNT),...]
    unnamed x10 -> x2, local copies, waits for them, and re-layouts: 5.26 us -> 2.36 us
where the time goes in v2:
time: 48.1 us; the launch traced here: 47.1 us
  Pallas kernels  44.1 us (92%)
  local copies, waits for them, and re-layouts  2.36 us (5%)
  between operations  0.64 us (1%)
    pallas_call x1, Pallas kernels, local(): pl.pallas_call(kernel, out_shape=(jax.ShapeDtypeStruct((1, 1, 2, COUNT),...  44.1 us
    unnamed x2, local copies, waits for them, and re-layouts  2.36 us

profile of v2, /device:TPU:1, one launch (start us, length us, event | category | flops | bytes accessed | tf_op | source)
XLA Modules:
  0.0 47.1 jit_solution(12230711229189731609)
XLA Ops:
  0.6 44.1 %patch_flow.1 = (f32[1,1,2,32]{3,2,1,0:T(2,128)}, f32[1,1,32]{2,1,0:T(1,128)}) custom-call(f32[1,1,256,512]{3,2,1,0:T(8,128)} %sec_ref.1, f32[1,448,704]{2,1,0:T(8,128)} %fol_ref.1, bf16[256,256]{1,0:T(8,128)(2,1)} %constant.6.clone.tc_ref, bf16[256,256]{1,0:T(8,128)(2,1)} %constant.7.clone.tr_ref, bf16[512,256]{1,0:T(8,128)(2,1)} %constant.8.clone.t4_ref), custom_call_target="tpu_custom_call" | custom-call | tf_op jit(solution)/shard_map/patch_flow/pallas_call | solution.py:425
  44.8 1.2 %copy.9 = f32[1,1,2,32]{3,2,1,0:T(2,128)} copy(f32[1,1,2,32]{3,2,1,0:T(2,128)} %get-tuple-element.4) | data formatting | bytes 512
  46.0 1.1 %copy.10 = f32[1,1,32]{2,1,0:T(1,128)} copy(f32[1,1,32]{2,1,0:T(1,128)} %get-tuple-element.5) | data formatting | bytes 256

commit v3 on v2

--- a/solution.py
+++ b/solution.py
@@ -115,16 +115,23 @@
     return [v.astype(BF16) for v in (xr + yr, xi + yi, xi - yi, yr - xr)]
 
 
-def patch_row(i, px, pcen, pinv, winv, tc, tr, t4, spec, peak):
-    rows = pl.ds(STRIDE * i, PATCH)
+def patch_moments(px, slot, base, pcen, pinv):
+    strips = [px[slot, pl.ds(pl.multiple_of(base + STRIDE * i, STRIDE), STRIDE), :] for i in range(3)]
+    mean, inverse = moments(strips, PATCH)
+    spread_out(mean, pcen, LANE - PM)
+    spread_out(inverse, pinv, LANE - PM)
+
+
+def patch_row(i, px, slot, m, pcen, pinv, winv, tc, tr, t4, spec, peak):
     offset = lax.broadcasted_iota(jnp.int32, (PATCH // 8, 8, PATCH), 0) * 8
     offset = offset + lax.broadcasted_iota(jnp.int32, (PATCH // 8, 8, PATCH), 1)
     offset = (offset - PATCH // 2).astype(F32)
-    band = px[rows, :]
+    band = px[slot, pl.ds(pl.multiple_of(STRIDE * i, STRIDE), PATCH), :]
+    at, one = pl.ds(m, 1), pl.ds(i, 1)
     x = []
     for j in range(8):
         lane = LANE - PM + STRIDE * j
-        x.append((band[:, lane:lane + PATCH] - pcen[j, i:i + 1, 0:1]).astype(BF16))
+        x.append((band[:, lane:lane + PATCH] - pcen[j, at, 0:1]).astype(BF16))
     a = dot(jnp.concatenate(x, 0), tc[:PATCH, :]).astype(BF16)
     fs = []
     for jj in range(4):
@@ -134,8 +141,8 @@
         fs.append(dot(t4[...], jnp.concatenate([upper, lower], 0)).astype(BF16))
     lhs = []
     for jj in range(4):
-        f = [fs[jj][LANE * m:LANE * m + LANE] for m in range(4)]
-        ar, ai, di, dr = cross(f, [spec[i * 4 + jj, m] for m in range(4)])
+        f = [fs[jj][LANE * n:LANE * n + LANE] for n in range(4)]
+        ar, ai, di, dr = cross(f, [spec[i * 4 + jj, n] for n in range(4)])
         for k in range(2):
             h = slice(LANE * k, LANE * k + LANE)
             lhs += [jnp.concatenate([ar[:, h], ai[:, h]], 1), jnp.concatenate([di[:, h], dr[:, h]], 1)]
@@ -144,7 +151,7 @@
         s = dot(tc[:PATCH, :], jnp.concatenate([uv[512 * jj:512 * jj + 256], uv[512 * jj + 256:512 * jj + 512]], 1))
         for k in range(2):
             j = 2 * jj + k
-            scale = pinv[j, i:i + 1, :] * winv[j, i:i + 1, :] * (1.0 / (32768.0 * 128.0))
+            scale = pinv[j, at, :] * winv[j, one, :] * (1.0 / (32768.0 * 128.0))
             score = (s[:, LANE * k:LANE * k + LANE] * scale).reshape(PATCH // 8, 8, PATCH)
             high = jnp.max(score, axis=0)
             weight = jnp.exp(score - high[None])
@@ -153,7 +160,7 @@
             peak[2, i * 8 + j] = jnp.sum(weight * offset, axis=0)
 
 
-def finish(peak, res):
+def finish(peak, res, slot):
     high = peak[0]
     top = jnp.max(jnp.max(high, axis=1, keepdims=True), axis=2, keepdims=True)
     scale = jnp.exp(high - top)
@@ -169,7 +176,7 @@
     strength = (top + jnp.log(whole)) * (1.0 / 128.0)
     place = lax.broadcasted_iota(jnp.int32, (COUNT, 1, LANE), 0) == lax.broadcasted_iota(jnp.int32, (COUNT, 1, LANE), 2)
     for k, v in enumerate((by_row, by_col, strength)):
-        res[k:k + 1, :] = jnp.sum(jnp.where(place, v, 0.0), axis=0)
+        res[slot, k:k + 1, :] = jnp.sum(jnp.where(place, v, 0.0), axis=0)
 
 
 def pack(x, lane):
@@ -194,65 +201,86 @@
     return pl.when(ok)
 
 
-def kernel(sec_ref, fol_ref, tc_ref, tr_ref, t4_ref, flow_ref, strength_ref,
+def kernel(sec_ref, fol_ref, tc_ref, tr_ref, t4_ref, out_ref,
            tc, tr, t4, wx, px, e0, e1, wcen, winv, pcen, pinv, spec, peak, out_cols, in_cols, res, res_in,
-           lsem, wsend, wrecv, fsend, frecv, psend, precv, csend, crecv, rsem):
+           lsem, wsend, wrecv, fsend, frecv, psend, precv, csend, crecv, rsem, grant_sem):
     s, t = lax.axis_index("sec"), lax.axis_index("tile")
     r, c = t // TCOLS, lax.rem(t, TCOLS)
     after, before = lax.rem(s + 1, SECS), lax.rem(s + SECS - 1, SECS)
     has_up, has_down, has_left, has_right = r > 0, r < TROWS - 1, c > 0, c < TCOLS - 1
     up, down, left, right = (s, t - TCOLS), (s, t + TCOLS), (s, t - 1), (s, t + 1)
-    first = s == 0
-    inner = jnp.logical_not(first)
+    first, last = s == 0, s == SECS - 1
+    inner = s > 0
+    even = lax.rem(s, 2) == 0
+    odd = jnp.logical_not(even)
+    taker = even & inner
+    sender = odd & jnp.logical_not(last)
+    eager = lax.rem(s // 2, 2) == 1
     sides = [(has_left, left), (has_right, right), (has_up, up), (has_down, down)]
+    near = sum(ok.astype(jnp.int32) for ok, _ in sides)
 
     barrier = pltpu.get_barrier_semaphore()
-    for d in ((after, t), (before, t)):
-        pl.semaphore_signal(barrier, inc=1, device_id=d, device_id_type=MESH)
-    for ok, d in sides:
+
+    def signal(sem, d):
+        pl.semaphore_signal(sem, inc=1, device_id=d, device_id_type=MESH)
+
+    evens = jnp.where(even, s, before)
+    for (ok, _), step in zip(sides, (-1, 1, -TCOLS, TCOLS)):
         @when(ok)
         def _():
-            pl.semaphore_signal(barrier, inc=1, device_id=d, device_id_type=MESH)
+            signal(barrier, (evens, t + step))
+
+    @when(inner)
+    def _():
+        signal(barrier, (before, t))
 
     own = sec_ref.at[0, 0]
-    constants = [pltpu.make_async_copy(a, b, lsem.at[1 + n]) for n, (a, b) in enumerate(((tc_ref, tc), (tr_ref, tr), (t4_ref, t4)))]
+    constants = [pltpu.make_async_copy(a, b, lsem.at[2 + n]) for n, (a, b) in enumerate(((tc_ref, tc), (tr_ref, tr), (t4_ref, t4)))]
     centre = pltpu.make_async_copy(own, wx.at[pl.ds(WM, TH), pl.ds(LANE, TW)], lsem.at[0])
-    spare = pltpu.make_async_copy(fol_ref.at[0], e0, lsem.at[0])
-
-    @when(inner)
-    def _():
-        centre.start()
-
-    @when(first)
+    spare = pltpu.make_async_copy(fol_ref.at[0], e0, lsem.at[1])
+    centre.start()
+
+    @when(last)
     def _():
         spare.start()
 
     for copy in constants:
         copy.start()
 
-    for buf, m in ((wx, WM), (px, PM)):
+    def clear(buf, at, m):
         rows = TH + 2 * m
 
         @when(jnp.logical_not(has_up))
         def _():
-            buf[0:m, :] = jnp.zeros((m, WIDE), F32)
+            buf[at + (pl.ds(0, m), slice(None))] = jnp.zeros((m, WIDE), F32)
 
         @when(jnp.logical_not(has_down))
         def _():
-            buf[m + TH:, :] = jnp.zeros((m, WIDE), F32)
+            buf[at + (pl.ds(m + TH, m), slice(None))] = jnp.zeros((m, WIDE), F32)
 
         @when(jnp.logical_not(has_left))
         def _():
-            buf[:, 0:LANE] = jnp.zeros((rows, LANE), F32)
+            buf[at + (slice(None), pl.ds(0, LANE))] = jnp.zeros((rows, LANE), F32)
 
         @when(jnp.logical_not(has_right))
         def _():
-            buf[:, LANE + TW:] = jnp.zeros((rows, LANE), F32)
-
-    res[...] = jnp.zeros((8, LANE), F32)
-
-    near = sum(ok.astype(jnp.int32) for ok, _ in sides)
-    pl.semaphore_wait(barrier, 2 + near)
+            buf[at + (slice(None), pl.ds(LANE + TW, LANE))] = jnp.zeros((rows, LANE), F32)
+
+    clear(wx, (), WM)
+
+    @when(taker)
+    def _():
+        clear(px, (0,), PM)
+
+    res[...] = jnp.zeros(res.shape, F32)
+
+    @when(even)
+    def _():
+        pl.semaphore_wait(barrier, 2 * near + 1)
+
+        @when(jnp.logical_not(eager))
+        def _():
+            signal(grant_sem, (after, t))
 
     def remote(src, dst, ssem, rsem, d):
         return pltpu.make_async_remote_copy(src_ref=src, dst_ref=dst, send_sem=ssem, recv_sem=rsem,
@@ -286,35 +314,74 @@
         (has_down, has_up, remote(own.at[pl.ds(TH - WM, WM)], wx.at[pl.ds(0, WM), pl.ds(LANE, TW)], wsend.at[3], wrecv.at[3], down)),
     ]
 
-    def corners(buf, m, ssem, rsem, base):
+    def corners(buf, at, m, ssem, rsem, base):
         out = []
         for i, (side, lane) in enumerate(((has_left, 0), (has_right, LANE + TW))):
-            lanes = pl.ds(lane, LANE)
+            def rows(a):
+                return buf.at[at + (pl.ds(a, m), pl.ds(lane, LANE))]
             out.append((side & has_up, side & has_down, remote(
-                buf.at[pl.ds(m, m), lanes], buf.at[pl.ds(m + TH, m), lanes], ssem.at[base + 2 * i], rsem.at[base + 2 * i], up)))
+                rows(m), rows(m + TH), ssem.at[base + 2 * i], rsem.at[base + 2 * i], up)))
             out.append((side & has_down, side & has_up, remote(
-                buf.at[pl.ds(TH, m), lanes], buf.at[pl.ds(0, m), lanes], ssem.at[base + 2 * i + 1], rsem.at[base + 2 * i + 1], down)))
+                rows(TH), rows(0), ssem.at[base + 2 * i + 1], rsem.at[base + 2 * i + 1], down)))
         return out
 
-    wcorners = corners(wx, WM, wsend, wrecv, 4)
+    wcorners = corners(wx, (), WM, wsend, wrecv, 4)
 
     ranges = [(0, PM), (TH - PM, PM)] + [(PM + STRIDE * n, STRIDE) for n in range(CUTS - 1)]
-    far = [remote(own.at[pl.ds(a, n)], px.at[pl.ds(PM + a, n), pl.ds(LANE, TW)], fsend.at[k], frecv.at[k], (after, t))
+    far = [remote(own.at[pl.ds(a, n)], px.at[0, pl.ds(PM + a, n), pl.ds(LANE, TW)], fsend.at[k], frecv.at[k], (after, t))
            for k, (a, n) in enumerate(ranges)]
-
-    @when(inner)
-    def _():
+    whole = remote(wx.at[pl.ds(WM - PM, PROWS)], px.at[0], fsend.at[CUTS + 1], frecv.at[CUTS + 1], (after, t))
+
+    def first_margins():
         start(wcols)
         start(wrows)
 
-    for copy in far:
-        copy.start()
+    def far_start(copies):
+        @when(sender)
+        def _():
+            for copy in copies:
+                copy.start()
+
+    def far_permission():
+        @when(sender)
+        def _():
+            pl.semaphore_wait(barrier, 1)
+
+    def second_margins():
+        wait_recv(wcols)
+        start(wcorners)
+
+    @when(even)
+    def _():
+        first_margins()
+        second_margins()
+
+        @when(eager)
+        def _():
+            signal(grant_sem, (after, t))
+
+    @when(odd & eager)
+    def _():
+        far_permission()
+        far_start(far[:3])
+        pl.semaphore_wait(grant_sem, 1)
+        first_margins()
+        far_start(far[3:])
+        second_margins()
+
+    @when(odd & jnp.logical_not(eager))
+    def _():
+        pl.semaphore_wait(grant_sem, 1)
+        first_margins()
+        far_permission()
+        far_start(far)
+        second_margins()
 
     prows = [
-        (has_up, has_down, remote(px.at[pl.ds(PM, PM), pl.ds(LANE, TW)], px.at[pl.ds(PM + TH, PM), pl.ds(LANE, TW)], psend.at[0], precv.at[0], up)),
-        (has_down, has_up, remote(px.at[pl.ds(TH, PM), pl.ds(LANE, TW)], px.at[pl.ds(0, PM), pl.ds(LANE, TW)], psend.at[1], precv.at[1], down)),
+        (has_up, has_down, remote(px.at[0, pl.ds(PM, PM), pl.ds(LANE, TW)], px.at[0, pl.ds(PM + TH, PM), pl.ds(LANE, TW)], psend.at[0], precv.at[0], up)),
+        (has_down, has_up, remote(px.at[0, pl.ds(TH, PM), pl.ds(LANE, TW)], px.at[0, pl.ds(0, PM), pl.ds(LANE, TW)], psend.at[1], precv.at[1], down)),
     ]
-    pcorners = corners(px, PM, psend, precv, 2)
+    pcorners = corners(px, (0,), PM, psend, precv, 2)
     pcols = [[
         (has_left, has_right, remote(out_cols.at[2 * n], in_cols.at[2 * n], csend.at[2 * n], crecv.at[2 * n], left)),
         (has_right, has_left, remote(out_cols.at[2 * n + 1], in_cols.at[2 * n + 1], csend.at[2 * n + 1], crecv.at[2 * n + 1], right)),
@@ -329,7 +396,7 @@
         for side, (ok, lane, at) in enumerate(((has_left, LANE, 0), (has_right, TW, LANE - PM))):
             @when(ok)
             def _():
-                x = jnp.concatenate([px[a:a + m, lane:lane + LANE] for a, m in part(n)], 0)
+                x = jnp.concatenate([px[0, a:a + m, lane:lane + LANE] for a, m in part(n)], 0)
                 out_cols[2 * n + side] = pack(x, at)
         start(pcols[n])
 
@@ -341,79 +408,150 @@
                 y = unpack(in_cols[2 * n + side], at)
                 b = 0
                 for a, m in part(n):
-                    px[a:a + m, lane:lane + LANE] = y[b:b + m]
+                    px[0, a:a + m, lane:lane + LANE] = y[b:b + m]
                     b += m
 
-    @when(inner)
-    def _():
-        wait_recv(wcols)
-        start(wcorners)
-
-    for k in range(2):
-        far[k].wait_recv()
-    start(prows)
-    send_cols(0)
-
-    @when(inner)
-    def _():
+    def far_take(n):
+        for k in ((0, 1) if n == 0 else (n + 1,)):
+            far[k].wait_recv()
+        if n == 0:
+            start(prows)
+        send_cols(n)
+
+    for copy in constants:
+        copy.wait()
+    centre.wait()
+
+    @when(taker)
+    def _():
+        far_take(0)
+
+    def extended():
         wait_recv(wrows)
         wait_recv(wcorners)
-        centre.wait()
-        e0[...] = wx[:, LANE - WM:LANE - WM + SPAN]
+
+        @when(even)
+        def _():
+            whole.start()
 
     @when(first)
     def _():
-        spare.wait()
-
-    e1[...] = e0[:, STRIDE:]
-    mean, inverse = moments(
-        [jnp.concatenate([e0[STRIDE * i:STRIDE * i + STRIDE, :], jnp.zeros((STRIDE, WIDE - SPAN), F32)], 1) for i in range(7)], WIN)
-    spread_out(mean, wcen, 0)
-    spread_out(inverse, winv, 0)
-
-    take_cols(0)
-    start(pcorners)
-    for copy in constants:
-        copy.wait()
-
-    def window_step(i, carry):
-        window_row(i, e0, e1, wcen, tc, tr, spec)
+        extended()
+
+    back = remote(res.at[1], res_in, rsem.at[0], rsem.at[1], (before, t))
+
+    def work(n, carry):
+        @when(n == 0)
+        def _():
+            spare.wait()
+
+        @when((n == 1) & jnp.logical_not(last))
+        def _():
+            extended()
+
+        @when(n == 1)
+        def _():
+            e0[...] = wx[:, LANE - WM:LANE - WM + SPAN]
+
+        e1[...] = e0[:, STRIDE:]
+        mean, inverse = moments(
+            [jnp.concatenate([e0[STRIDE * i:STRIDE * i + STRIDE, :], jnp.zeros((STRIDE, WIDE - SPAN), F32)], 1) for i in range(7)], WIN)
+        spread_out(mean, wcen, 0)
+        spread_out(inverse, winv, 0)
+
+        def window_step(i, inside):
+            for at in (1, 2):
+                @when(taker & (i == 2 * at - 1))
+                def _():
+                    far_take(at)
+
+            window_row(i, e0, e1, wcen, tc, tr, spec)
+            return inside
+
+        lax.fori_loop(0, 4, window_step, 0)
+
+        @when(n == 0)
+        def _():
+            extended()
+            px[1] = wx[WM - PM:WM - PM + PROWS, :]
+
+        @when((n == 1) & odd)
+        def _():
+            whole.wait_recv()
+
+        @when(taker)
+        def _():
+            take_cols(0)
+            start(pcorners)
+            take_cols(1)
+            take_cols(2)
+            wait_recv(prows)
+            wait_recv(pcorners)
+
+        def phase(h, inside):
+            @when(taker & (h == 1))
+            def _():
+                take_cols(3)
+
+            patch_moments(px, 1 - n, 2 * STRIDE * h, pcen, pinv)
+
+            def patch_step(m, deeper):
+                @when(taker & (h == 0) & (m == 1))
+                def _():
+                    far_take(3)
+
+                patch_row(2 * h + m, px, 1 - n, m, pcen, pinv, winv, tc, tr, t4, spec, peak)
+                return deeper
+
+            return lax.fori_loop(0, 2, patch_step, inside)
+
+        lax.fori_loop(0, 2, phase, 0)
+        finish(peak, res, n)
         return carry
 
-    lax.fori_loop(0, 4, window_step, 0)
-
-    for n in range(1, CUTS):
-        far[n + 1].wait_recv()
-        send_cols(n)
-        if n > 1:
-            take_cols(n - 1)
-    wait_recv(prows)
-    wait_recv(pcorners)
-    take_cols(CUTS - 1)
-    mean, inverse = moments([px[STRIDE * i:STRIDE * i + STRIDE, :] for i in range(5)], PATCH)
-    spread_out(mean, pcen, LANE - PM)
-    spread_out(inverse, pinv, LANE - PM)
-    for i in range(4):
-        patch_row(i, px, pcen, pinv, winv, tc, tr, t4, spec, peak)
-    finish(peak, res)
-    back = remote(res, res_in, rsem.at[0], rsem.at[1], (before, t))
-    back.start()
+    lax.fori_loop(jnp.where(last, 0, jnp.where(first, 2, 1)), 2, work, 0)
 
     @when(inner)
     def _():
-        wait_send(wcols)
-        wait_send(wrows)
-        wait_send(wcorners)
-
-    for copy in far:
-        copy.wait_send()
-    wait_send(prows)
-    wait_send(pcorners)
-    for copies in pcols:
-        wait_send(copies)
-    back.wait()
-    flow_ref[0, 0] = res_in[0:2, 0:COUNT]
-    strength_ref[0] = res_in[2:3, 0:COUNT]
+        back.start()
+
+    wait_send(wcols)
+    wait_send(wrows)
+    wait_send(wcorners)
+
+    @when(taker)
+    def _():
+        wait_send(prows)
+        wait_send(pcorners)
+        for copies in pcols:
+            wait_send(copies)
+
+    @when(sender)
+    def _():
+        for copy in far:
+            copy.wait_send()
+
+    @when(even)
+    def _():
+        whole.wait_send()
+
+    @when(inner)
+    def _():
+        back.wait_send()
+
+    @when(last)
+    def _():
+        out_ref[0] = res[0]
+
+    @when(jnp.logical_not(last))
+    def _():
+        back.wait_recv()
+        out_ref[0] = res_in[...]
+
+
+def place(in_ref, flow_ref, strength_ref):
+    flow_ref[0, 0] = in_ref[0, 0:2, 0:COUNT]
+    strength_ref[0] = in_ref[0, 2:3, 0:COUNT]
 
 
 def solution(mesh):
@@ -422,15 +560,15 @@
     def local(sections, following):
         dma = pltpu.SemaphoreType.DMA
         vmem = pltpu.VMEM
-        return pl.pallas_call(
+        found = pl.pallas_call(
             kernel,
-            out_shape=(jax.ShapeDtypeStruct((1, 1, 2, COUNT), F32), jax.ShapeDtypeStruct((1, 1, COUNT), F32)),
+            out_shape=jax.ShapeDtypeStruct((1, 8, LANE), F32),
             in_specs=[pl.BlockSpec(memory_space=pl.ANY)] * 5,
-            out_specs=(pl.BlockSpec(memory_space=vmem),) * 2,
+            out_specs=pl.BlockSpec(memory_space=vmem),
             scratch_shapes=[
                 vmem((WIN, WIN), BF16), vmem((WIN, WIN), BF16), vmem((2 * WIN, WIN), BF16),
                 vmem((WROWS, WIDE), F32),
-                vmem((PROWS, WIDE), F32),
+                vmem((2, PROWS, WIDE), F32),
                 vmem((WROWS, SPAN), F32),
                 vmem((WROWS, SPAN - STRIDE), F32),
                 vmem((8, 8, LANE), F32), vmem((8, 8, LANE), F32), vmem((8, 8, LANE), F32), vmem((8, 8, LANE), F32),
@@ -438,14 +576,22 @@
                 vmem((3, COUNT, 8, LANE), F32),
                 vmem((2 * CUTS, 16, LANE), F32),
                 vmem((2 * CUTS, 16, LANE), F32),
+                vmem((2, 8, LANE), F32),
                 vmem((8, LANE), F32),
-                vmem((8, LANE), F32),
-                dma((4,)), dma((8,)), dma((8,)), dma((CUTS + 1,)), dma((CUTS + 1,)),
+                dma((5,)), dma((8,)), dma((8,)), dma((CUTS + 2,)), dma((CUTS + 2,)),
                 dma((6,)), dma((6,)), dma((2 * CUTS,)), dma((2 * CUTS,)), dma((2,)),
+                pltpu.SemaphoreType.REGULAR,
             ],
             compiler_params=pltpu.CompilerParams(collective_id=0, has_side_effects=True, vmem_limit_bytes=58 * 2**20),
             name="patch_flow",
         )(sections, following, *[jnp.asarray(v) for v in tabs])
+        return tuple(pl.pallas_call(
+            place,
+            out_shape=(jax.ShapeDtypeStruct((1, 1, 2, COUNT), F32), jax.ShapeDtypeStruct((1, 1, COUNT), F32)),
+            in_specs=[pl.BlockSpec(memory_space=vmem)],
+            out_specs=(pl.BlockSpec(memory_space=vmem),) * 2,
+            name="place",
+        )(found))
 
     return jax.shard_map(
         local,

time: 48.1 us -> 45.7 us (0.950); the launches traced: 47.1 us -> 45.6 us
  local copies, waits for them, and re-layouts: 2.36 us -> 0 us
  Pallas kernels: 44.1 us -> 45 us
    unnamed x2 -> x0, local copies, waits for them, and re-layouts: 2.36 us -> none
    pallas_call x1 -> x2, Pallas kernels: 44.1 us -> 45 us  [the longest x1 43.7 us: local(): pl.pallas_call(kernel, out_shape=jax.ShapeDtypeStruct((1, 8, LANE), F32),...]
where the time goes in v3:
time: 45.7 us; the launch traced here: 45.6 us
  Pallas kernels  45 us (98%)
  between operations  0.64 us (1%)
    pallas_call x1, Pallas kernels, local(): pl.pallas_call(kernel, out_shape=jax.ShapeDtypeStruct((1, 8, LANE), F32),...  43.7 us
    pallas_call x1, Pallas kernels, local(): pl.pallas_call(place, out_shape=(jax.ShapeDtypeStruct((1, 1, 2, COUNT), F...  1.25 us

profile of v3, /device:TPU:1, one launch (start us, length us, event | category | flops | bytes accessed | tf_op | source)
XLA Modules:
  0.0 45.6 jit_solution(17655500310669559345)
XLA Ops:
  0.6 43.7 %patch_flow.1.in_ref = f32[1,8,128]{2,1,0:T(8,128)} custom-call(f32[1,1,256,512]{3,2,1,0:T(8,128)} %sec_ref.1, f32[1,448,704]{2,1,0:T(8,128)} %fol_ref.1, bf16[256,256]{1,0:T(8,128)(2,1)} %constant.6.clone.tc_ref, bf16[256,256]{1,0:T(8,128)(2,1)} %constant.7.clone.tr_ref, bf16[512,256]{1,0:T(8,128)(2,1)} %constant.8.clone.t4_ref), custom_call_target="tpu_custom_call" | custom-call | tf_op jit(solution)/shard_map/patch_flow/pallas_call | solution.py:563
  44.4 1.2 %place.1 = (f32[1,1,2,32]{3,2,1,0:T(2,128)}, f32[1,1,32]{2,1,0:T(1,128)}) custom-call(f32[1,8,128]{2,1,0:T(8,128)} %patch_flow.1.in_ref), custom_call_target="tpu_custom_call" | custom-call | tf_op jit(solution)/shard_map/place/pallas_call | solution.py:588

commit v4 on v3

v4 whole, which is shorter than its diff:
```python
import jax
import jax.numpy as jnp
import ml_dtypes
import numpy as np
from jax import lax
from jax.experimental import pallas as pl
from jax.experimental.pallas import tpu as pltpu
from jax.sharding import PartitionSpec as P

MESH = pl.DeviceIdType.MESH
F32 = jnp.float32
BF16 = jnp.bfloat16

PATCH = 128
WIN = 256
TH = 256
TW = 512
TCOLS = 4
TROWS = 4
SECS = 16
STRIDE = 64
WM = 96
PM = 32
LANE = 128
WROWS = TH + 2 * WM
PROWS = TH + 2 * PM
WIDE = TW + 2 * LANE
SPAN = TW + 2 * WM
COUNT = 32


def tables():
    b = np.arange(WIN)[:, None]
    turn = (b * (2 * np.arange(PATCH)[None, :] + 1)) % (2 * WIN)
    angle = turn * (np.pi / WIN)
    tc = np.concatenate([np.cos(angle), np.sin(angle)], 1)
    cr, sr = tc[:PATCH, :PATCH].T, tc[:PATCH, PATCH:].T
    four = np.concatenate([np.concatenate(x, 1) for x in ((cr, -sr), (sr, cr), (cr, sr), (-sr, cr))], 0)
    return [np.ascontiguousarray(v).astype(np.float32).astype(ml_dtypes.bfloat16) for v in (tc, tc.T, four)]


def dot(a, b):
    return jnp.dot(a, b, preferred_element_type=F32)


def tree(x):
    rows = x.shape[0]
    while rows > 8:
        rows //= 2
        x = x[:rows] + x[rows:]
    for h in (4, 2, 1):
        x = x + pltpu.roll(x, h, 0)
    return x


def fold(x):
    rows = x.shape[0]
    while rows > 8:
        rows //= 2
        x = x[:rows] + x[rows:]
    return sum((x[:, a:a + LANE] for a in range(LANE, x.shape[1], LANE)), x[:, :LANE])


def total(x):
    return jnp.sum(jnp.sum(x, axis=-2, keepdims=True), axis=-1, keepdims=True)


def inner_centres(wx, slot, wcen):
    strips = [tree(wx[slot, STRIDE * i:STRIDE * i + STRIDE, LANE:LANE + TW]) for i in (2, 3, 4)]
    middle = strips[0] + strips[1] + strips[2]
    sub = lax.broadcasted_iota(jnp.int32, middle.shape, 0)
    sums = jnp.where(sub == 0, middle - strips[2], jnp.where(sub == 3, middle - strips[0], middle))
    h = 1
    while h < STRIDE:
        sums = sums + pltpu.roll(sums, TW - h, 1)
        h *= 2
    rows = jnp.where((sub == 0) | (sub == 3), 2.0 * STRIDE, 3.0 * STRIDE)[:, 0:1]
    blocks = [sums[:, PM + STRIDE * m:PM + STRIDE * m + 1] for m in range(7)]
    for j in range(8):
        part = blocks[max(0, j - 2):min(7, j + 2)]
        wcen[j] = jnp.broadcast_to(sum(part[1:], part[0]) / (rows * float(STRIDE * len(part))), (8, LANE))


def window_row(i, wx, slot, cen, sums, tc, tr, spec):
    rows = pl.ds(pl.multiple_of(i * STRIDE, STRIDE), WIN)
    for j in range(8):
        lane = LANE - WM + STRIDE * j
        x = wx[slot, rows, pl.ds(lane // LANE * LANE, WIN + LANE)][:, lane % LANE:lane % LANE + WIN]
        x = x - cen[j, pl.ds(i, 1), 0:1]
        sums[0, i * 8 + j] = fold(x)
        sums[1, i * 8 + j] = fold(x * x)
        z = dot(tr[...], dot(x.astype(BF16), tc[...]).astype(BF16))
        p, r = z[:PATCH, :PATCH], z[:PATCH, PATCH:]
        t, q = z[PATCH:, :PATCH], z[PATCH:, PATCH:]
        for m, g in enumerate((p - q, r + t, p + q, r - t)):
            spec[i * 4 + j // 2, m, :, pl.ds(LANE * (j % 2), LANE)] = g.astype(BF16)


def cross(f, g):
    xr = f[0] * g[0] + f[1] * g[1]
    xi = f[0] * g[1] - f[1] * g[0]
    yr = f[2] * g[2] + f[3] * g[3]
    yi = f[2] * g[3] - f[3] * g[2]
    return [xr + yr, xi + yi, xi - yi, yr - xr]


def window_scales(sums, winv):
    mean = total(sums[0]) * (1.0 / (WIN * WIN))
    spread = total(sums[1]) * (1.0 / (WIN * WIN)) - mean * mean
    winv[...] = jnp.broadcast_to(lax.rsqrt(jnp.maximum(spread, 0.0) + 1e-5), winv.shape)


def patch_row(i, px, slot, winv, tc, tr, t4, spec, peak):
    offset = lax.broadcasted_iota(jnp.int32, (PATCH // 8, 8, PATCH), 0) * 8
    offset = offset + lax.broadcasted_iota(jnp.int32, (PATCH // 8, 8, PATCH), 1)
    offset = (offset - PATCH // 2).astype(F32)
    band = px[slot, pl.ds(pl.multiple_of(STRIDE * i, STRIDE), PATCH), :]
    x = [band[:, LANE - PM + STRIDE * j:LANE - PM + STRIDE * j + PATCH] for j in range(8)]
    centres = [total(fold(v)) * (1.0 / (PATCH * PATCH)) for v in x]
    x = [v - m for v, m in zip(x, centres)]
    scales = []
    for j in range(8):
        spread = total(fold(x[j] * x[j])) * (1.0 / (PATCH * PATCH))
        scales.append(lax.rsqrt(spread + 1e-5) * winv[i * 8 + j] * (1.0 / (32768.0 * 128.0)))
    x = [v.astype(BF16) for v in x]
    a = dot(jnp.concatenate(x, 0), tc[:PATCH, :]).astype(BF16)
    fs = []
    for jj in range(4):
        e, o = a[256 * jj:256 * jj + 128], a[256 * jj + 128:256 * jj + 256]
        upper = jnp.concatenate([e[:, :LANE], o[:, :LANE]], 1)
        lower = jnp.concatenate([e[:, LANE:], o[:, LANE:]], 1)
        fs.append(dot(t4[...], jnp.concatenate([upper, lower], 0)).astype(BF16))
    lhs = []
    for jj in range(4):
        f = [fs[jj][LANE * n:LANE * n + LANE] for n in range(4)]
        ar, ai, di, dr = cross(f, [spec[i * 4 + jj, n] for n in range(4)])
        for k in range(2):
            h = slice(LANE * k, LANE * k + LANE)
            lhs += [jnp.concatenate([ar[:, h], ai[:, h]], 1), jnp.concatenate([di[:, h], dr[:, h]], 1)]
    uv = dot(jnp.concatenate(lhs, 0), tr[:, :PATCH]).astype(BF16)
    for jj in range(4):
        s = dot(tc[:PATCH, :], jnp.concatenate([uv[512 * jj:512 * jj + 256], uv[512 * jj + 256:512 * jj + 512]], 1))
        for k in range(2):
            j = 2 * jj + k
            score = s[:, LANE * k:LANE * k + LANE].reshape(PATCH // 8, 8, PATCH) * scales[j]
            high = jnp.max(score, axis=0)
            weight = jnp.exp(score - high[None])
            peak[0, i * 8 + j] = high
            peak[1, i * 8 + j] = jnp.sum(weight, axis=0)
            peak[2, i * 8 + j] = jnp.sum(weight * offset, axis=0)


def finish(peak, res, slot):
    high = peak[0]
    top = jnp.max(jnp.max(high, axis=1, keepdims=True), axis=2, keepdims=True)
    scale = jnp.exp(high - top)
    weight = peak[1] * scale
    column = (lax.broadcasted_iota(jnp.int32, (COUNT, 8, LANE), 2) - PATCH // 2).astype(F32)

    whole = total(weight)
    by_row = total(peak[2] * scale) / whole
    by_col = total(weight * column) / whole
    strength = (top + jnp.log(whole)) * (1.0 / 128.0)
    place = lax.broadcasted_iota(jnp.int32, (COUNT, 1, LANE), 0) == lax.broadcasted_iota(jnp.int32, (COUNT, 1, LANE), 2)
    for k, v in enumerate((by_row, by_col, strength)):
        res[slot, k:k + 1, :] = jnp.sum(jnp.where(place, v, 0.0), axis=0)


def pack(x, lane):
    group = lax.broadcasted_iota(jnp.int32, (16, LANE), 1) // PM
    out = jnp.zeros((16, LANE), F32)
    for g in range(4):
        part = x[16 * g:16 * g + 16]
        shift = (PM * g - lane) % LANE
        out = jnp.where(group == g, pltpu.roll(part, shift, 1) if shift else part, out)
    return out


def unpack(y, lane):
    out = []
    for g in range(4):
        shift = (lane - PM * g) % LANE
        out.append(pltpu.roll(y, shift, 1) if shift else y)
    return jnp.concatenate(out, 0)


def when(ok):
    return pl.when(ok)


def kernel(sec_ref, fol_ref, tc_ref, tr_ref, t4_ref, out_ref,
           tc, tr, t4, wx, px, e0, wcen, sums, winv, spec, peak, out_cols, in_cols, res, res_in,
           lsem, wsend, wrecv, fsend, frecv, psend, precv, rsem, grant_sem):
    s, t = lax.axis_index("sec"), lax.axis_index("tile")
    r, c = t // TCOLS, lax.rem(t, TCOLS)
    after, before = lax.rem(s + 1, SECS), lax.rem(s + SECS - 1, SECS)
    has_up, has_down, has_left, has_right = r > 0, r < TROWS - 1, c > 0, c < TCOLS - 1
    left, right = (s, t - 1), (s, t + 1)
    first, last = s == 0, s == SECS - 1
    inner = s > 0
    even = lax.rem(s, 2) == 0
    odd = jnp.logical_not(even)
    taker = even & inner
    sender = odd & jnp.logical_not(last)
    eager = lax.rem(s // 2, 2) == 1
    steps = [(has_left, -1), (has_right, 1), (has_up, -TCOLS), (has_down, TCOLS)]
    steps += [(a & b, m + n) for a, m in steps[:2] for b, n in steps[2:]]
    near = sum(ok.astype(jnp.int32) for ok, _ in steps)

    barrier = pltpu.get_barrier_semaphore()

    def signal(sem, d):
        pl.semaphore_signal(sem, inc=1, device_id=d, device_id_type=MESH)

    evens = jnp.where(even, s, before)
    for ok, step in steps:
        @when(ok)
        def _():
            signal(barrier, (evens, t + step))

    @when(inner)
    def _():
        signal(barrier, (before, t))

    own = sec_ref.at[0, 0]
    constants = [pltpu.make_async_copy(a, b, lsem.at[2 + n]) for n, (a, b) in enumerate(((tc_ref, tc), (tr_ref, tr), (t4_ref, t4)))]
    centre = pltpu.make_async_copy(own, wx.at[0, pl.ds(WM, TH), pl.ds(LANE, TW)], lsem.at[0])
    spare = pltpu.make_async_copy(fol_ref.at[0], e0, lsem.at[1])
    centre.start()

    @when(last)
    def _():
        spare.start()

    for copy in constants:
        copy.start()

    @when(jnp.logical_not(has_up))
    def _():
        wx[0, 0:WM, :] = jnp.zeros((WM, WIDE), F32)

        @when(taker)
        def _():
            px[0, 0:PM, LANE:LANE + TW] = jnp.zeros((PM, TW), F32)

    @when(jnp.logical_not(has_down))
    def _():
        wx[0, WM + TH:, :] = jnp.zeros((WM, WIDE), F32)

        @when(taker)
        def _():
            px[0, PM + TH:, LANE:LANE + TW] = jnp.zeros((PM, TW), F32)

    @when(jnp.logical_not(has_left))
    def _():
        wx[0, :, 0:LANE] = jnp.zeros((WROWS, LANE), F32)

    @when(jnp.logical_not(has_right))
    def _():
        wx[0, :, LANE + TW:] = jnp.zeros((WROWS, LANE), F32)

    res[...] = jnp.zeros(res.shape, F32)

    @when(even)
    def _():
        pl.semaphore_wait(barrier, 2 * near + 1)

        @when(jnp.logical_not(eager))
        def _():
            signal(grant_sem, (after, t))

    def remote(src, dst, ssem, rsem, d):
        return pltpu.make_async_remote_copy(src_ref=src, dst_ref=dst, send_sem=ssem, recv_sem=rsem,
                                            device_id=d, device_id_type=MESH)

    def start(copies):
        for ok, _, copy in copies:
            @when(ok)
            def _():
                copy.start()

    def wait_recv(copies):
        for _, ok, copy in copies:
            @when(ok)
            def _():
                copy.wait_recv()

    def wait_send(copies):
        for ok, _, copy in copies:
            @when(ok)
            def _():
                copy.wait_send()

    def ring(src, at, buf, to, m, ssem, rsem, base):
        r0, c0 = at
        out = []
        edge = c0 + TW - LANE
        for k, (vert, opposite, row, dst, step) in enumerate((
                (has_up, has_down, r0, m + TH, -TCOLS), (has_down, has_up, r0 + TH - m, 0, TCOLS))):
            for n, (side, other, lane, width, dlane, move) in enumerate((
                    (None, None, c0, TW, LANE, 0), (has_left, has_right, c0, LANE, LANE + TW, -1), (has_right, has_left, edge, LANE, 0, 1))):
                sends = vert if side is None else vert & side
                takes = opposite if side is None else opposite & other
                out.append((sends, takes, remote(
                    src.at[pl.ds(row, m), pl.ds(lane, width)], buf.at[to, pl.ds(dst, m), pl.ds(dlane, width)],
                    ssem.at[base + 3 * k + n], rsem.at[base + 3 * k + n], (s, t + step + move))))
        return out

    edge = TW - LANE
    wmargins = ring(own, (0, 0), wx, 0, WM, wsend, wrecv, 2)
    wmargins = [
        (has_left, has_right, remote(own.at[:, pl.ds(0, LANE)], wx.at[0, pl.ds(WM, TH), pl.ds(LANE + TW, LANE)], wsend.at[0], wrecv.at[0], left)),
        (has_right, has_left, remote(own.at[:, pl.ds(edge, LANE)], wx.at[0, pl.ds(WM, TH), pl.ds(0, LANE)], wsend.at[1], wrecv.at[1], right)),
    ] + wmargins

    ranges = [(0, PM), (TH - PM, PM)] + [(PM + STRIDE * n, STRIDE) for n in range(3)]
    pieces = [(own.at[pl.ds(a, n)], px.at[0, pl.ds(PM + a, n), pl.ds(LANE, TW)]) for a, n in ranges]
    pieces += [(out_cols.at[pl.ds(a, n)], in_cols.at[pl.ds(a, n)]) for a, n in ((0, 6), (6, 4))]
    far = [remote(a, b, fsend.at[k], frecv.at[k], (after, t)) for k, (a, b) in enumerate(pieces)]
    whole = remote(wx.at[0, pl.ds(WM - PM, PROWS)], px.at[0], fsend.at[7], frecv.at[7], (after, t))

    def far_start(copies):
        @when(sender)
        def _():
            for copy in copies:
                copy.start()

    def far_permission():
        @when(sender)
        def _():
            pl.semaphore_wait(barrier, 1)

    @when(even)
    def _():
        start(wmargins)

    @when(odd & jnp.logical_not(last))
    def _():
        pl.semaphore_wait(grant_sem, 1)
        start(wmargins)
        far_permission()
        far_start(far[:4])

    pmargins = [
        (has_up, has_down, remote(px.at[0, pl.ds(PM, PM), pl.ds(LANE, TW)], px.at[0, pl.ds(PM + TH, PM), pl.ds(LANE, TW)], psend.at[0], precv.at[0], (s, t - TCOLS))),
        (has_down, has_up, remote(px.at[0, pl.ds(TH, PM), pl.ds(LANE, TW)], px.at[0, pl.ds(0, PM), pl.ds(LANE, TW)], psend.at[1], precv.at[1], (s, t + TCOLS))),
    ]

    def send_cols():
        for k in range(5):
            row = WM - PM + STRIDE * k
            out_cols[2 * k] = pack(wx[0, row:row + STRIDE, 0:LANE], LANE - PM)
            out_cols[2 * k + 1] = pack(wx[0, row:row + STRIDE, LANE + TW:], 0)
        far_start([far[5], far[4], far[6]])

    def take_cols(strips):
        for k in strips:
            row = STRIDE * k
            px[0, row:row + STRIDE, 0:LANE] = unpack(in_cols[2 * k], LANE - PM)
            px[0, row:row + STRIDE, LANE + TW:] = unpack(in_cols[2 * k + 1], 0)

    def far_take(numbers):
        for k in numbers:
            far[k].wait_recv()

    for copy in constants:
        copy.wait()
    centre.wait()

    def extended():
        wait_recv(wmargins)

        @when(even)
        def _():
            whole.start()

        @when(even & eager)
        def _():
            signal(grant_sem, (after, t))

    @when(first)
    def _():
        extended()

    back = remote(res.at[1], res_in, rsem.at[0], rsem.at[1], (before, t))

    def work(n, carry):
        slot = 1 - n

        @when(n == 0)
        def _():
            spare.wait()
            wx[1] = jnp.concatenate([jnp.zeros((WROWS, PM), F32), e0[...], jnp.zeros((WROWS, PM), F32)], 1)

        inner_centres(wx, slot, wcen)

        @when((n == 1) & jnp.logical_not(last))
        def _():
            extended()

        @when(sender)
        def _():
            send_cols()

        def window_step(i, inside):
            @when(taker & (i == 2))
            def _():
                far_take((0, 1))
                start(pmargins)

            window_row(i, wx, slot, wcen, sums, tc, tr, spec)
            return inside

        lax.fori_loop(0, 4, window_step, 0)

        @when(n == 0)
        def _():
            pl.semaphore_wait(grant_sem, 1)
            start(wmargins)
            extended()
            px[1] = wx[0, WM - PM:WM - PM + PROWS, :]

        window_scales(sums, winv)

        @when((n == 1) & odd)
        def _():
            whole.wait_recv()

        @when(taker)
        def _():
            far_take((2, 3, 5))
            take_cols((0, 1, 2))
            wait_recv(pmargins)

        def phase(h, inside):
            @when(taker & (h == 1))
            def _():
                far_take((4, 6))
                take_cols((3, 4))

            def patch_step(m, deeper):
                patch_row(2 * h + m, px, 1 - n, winv, tc, tr, t4, spec, peak)
                return deeper

            return lax.fori_loop(0, 2, patch_step, inside)

        lax.fori_loop(0, 2, phase, 0)
        finish(peak, res, n)
        return carry

    lax.fori_loop(jnp.where(last, 0, jnp.where(first, 2, 1)), 2, work, 0)

    @when(inner)
    def _():
        back.start()

    wait_send(wmargins)

    @when(taker)
    def _():
        wait_send(pmargins)

    @when(sender)
    def _():
        for copy in far:
            copy.wait_send()

    @when(even)
    def _():
        whole.wait_send()

    @when(inner)
    def _():
        back.wait_send()

    @when(last)
    def _():
        out_ref[0] = res[0]

    @when(jnp.logical_not(last))
    def _():
        back.wait_recv()
        out_ref[0] = res_in[...]


def place(in_ref, flow_ref, strength_ref):
    flow_ref[0, 0] = in_ref[0, 0:2, 0:COUNT]
    strength_ref[0] = in_ref[0, 2:3, 0:COUNT]


def solution(mesh):
    tabs = tables()

    def local(sections, following):
        dma = pltpu.SemaphoreType.DMA
        vmem = pltpu.VMEM
        found = pl.pallas_call(
            kernel,
            out_shape=jax.ShapeDtypeStruct((1, 8, LANE), F32),
            in_specs=[pl.BlockSpec(memory_space=pl.ANY)] * 5,
            out_specs=pl.BlockSpec(memory_space=vmem),
            scratch_shapes=[
                vmem((WIN, WIN), BF16), vmem((WIN, WIN), BF16), vmem((2 * WIN, WIN), BF16),
                vmem((2, WROWS, WIDE), F32),
                vmem((2, PROWS, WIDE), F32),
                vmem((WROWS, SPAN), F32),
                vmem((8, 8, LANE), F32),
                vmem((2, COUNT, 8, LANE), F32),
                vmem((COUNT, 1, LANE), F32),
                vmem((16, 4, PATCH, WIN), BF16),
                vmem((3, COUNT, 8, LANE), F32),
                vmem((10, 16, LANE), F32),
                vmem((10, 16, LANE), F32),
                vmem((2, 8, LANE), F32),
                vmem((8, LANE), F32),
                dma((5,)), dma((8,)), dma((8,)), dma((8,)), dma((8,)), dma((2,)), dma((2,)), dma((2,)),
                pltpu.SemaphoreType.REGULAR,
            ],
            compiler_params=pltpu.CompilerParams(collective_id=0, has_side_effects=True, vmem_limit_bytes=58 * 2**20),
            name="patch_flow",
        )(sections, following, *[jnp.asarray(v) for v in tabs])
        return tuple(pl.pallas_call(
            place,
            out_shape=(jax.ShapeDtypeStruct((1, 1, 2, COUNT), F32), jax.ShapeDtypeStruct((1, 1, COUNT), F32)),
            in_specs=[pl.BlockSpec(memory_space=vmem)],
            out_specs=(pl.BlockSpec(memory_space=vmem),) * 2,
            name="place",
        )(found))

    return jax.shard_map(
        local,
        mesh=mesh,
        in_specs=(P("sec", "tile", None, None), P("tile", None, None)),
        out_specs=(P("sec", "tile", None, None), P("sec", "tile", None)),
        check_vma=False,
    )
```

time: 45.7 us -> 42.4 us (0.928)
  the two profiles are of different devices: /device:TPU:1 before, /device:TPU:14 now
where the time goes in v4:
time: 42.4 us; the launch traced here: 42.3 us
  Pallas kernels  41.7 us (98%)
  between operations  0.64 us (2%)
    pallas_call x1, Pallas kernels, local(): pl.pallas_call(kernel, out_shape=jax.ShapeDtypeStruct((1, 8, LANE), F32),...  40.4 us
    pallas_call x1, Pallas kernels, local(): pl.pallas_call(place, out_shape=(jax.ShapeDtypeStruct((1, 1, 2, COUNT), F...  1.25 us

profile of v4, /device:TPU:14, one launch (start us, length us, event | category | flops | bytes accessed | tf_op | source)
XLA Modules:
  0.0 42.3 jit_solution(16633039962035929414)
XLA Ops:
  0.6 40.4 %patch_flow.1.in_ref = f32[1,8,128]{2,1,0:T(8,128)} custom-call(f32[1,1,256,512]{3,2,1,0:T(8,128)} %sec_ref.1, f32[1,448,704]{2,1,0:T(8,128)} %fol_ref.1, bf16[256,256]{1,0:T(8,128)(2,1)} %constant.6.clone.tc_ref, bf16[256,256]{1,0:T(8,128)(2,1)} %constant.7.clone.tr_ref, bf16[512,256]{1,0:T(8,128)(2,1)} %constant.8.clone.t4_ref), custom_call_target="tpu_custom_call" | custom-call | tf_op jit(solution)/shard_map/patch_flow/pallas_call | solution.py:497
  41.0 1.2 %place.1 = (f32[1,1,2,32]{3,2,1,0:T(2,128)}, f32[1,1,32]{2,1,0:T(1,128)}) custom-call(f32[1,8,128]{2,1,0:T(8,128)} %patch_flow.1.in_ref), custom_call_target="tpu_custom_call" | custom-call | tf_op jit(solution)/shard_map/place/pallas_call | solution.py:522

commit v5 on v4

--- a/solution.py
+++ b/solution.py
@@ -265,9 +265,7 @@
     def _():
         pl.semaphore_wait(barrier, 2 * near + 1)
 
-        @when(jnp.logical_not(eager))
-        def _():
-            signal(grant_sem, (after, t))
+        signal(grant_sem, (after, t))
 
     def remote(src, dst, ssem, rsem, d):
         return pltpu.make_async_remote_copy(src_ref=src, dst_ref=dst, send_sem=ssem, recv_sem=rsem,
@@ -373,10 +371,6 @@
         @when(even)
         def _():
             whole.start()
-
-        @when(even & eager)
-        def _():
-            signal(grant_sem, (after, t))
 
     @when(first)
     def _():

time: 42.4 us -> 39.1 us (0.922)
  the two profiles are of different devices: /device:TPU:14 before, /device:TPU:69 now
where the time goes in v5:
time: 39.1 us; the launch traced here: 39 us
  Pallas kernels  38.3 us (98%)
  between operations  0.64 us (2%)
    pallas_call x1, Pallas kernels, local(): pl.pallas_call(kernel, out_shape=jax.ShapeDtypeStruct((1, 8, LANE), F32),...  37.1 us
    pallas_call x1, Pallas kernels, local(): pl.pallas_call(place, out_shape=(jax.ShapeDtypeStruct((1, 1, 2, COUNT), F...  1.25 us

profile of v5, /device:TPU:69, one launch (start us, length us, event | category | flops | bytes accessed | tf_op | source)
XLA Modules:
  0.0 39.0 jit_solution(7945068595200699031)
XLA Ops:
  0.6 37.1 %patch_flow.1.in_ref = f32[1,8,128]{2,1,0:T(8,128)} custom-call(f32[1,1,256,512]{3,2,1,0:T(8,128)} %sec_ref.1, f32[1,448,704]{2,1,0:T(8,128)} %fol_ref.1, bf16[256,256]{1,0:T(8,128)(2,1)} %constant.6.clone.tc_ref, bf16[256,256]{1,0:T(8,128)(2,1)} %constant.7.clone.tr_ref, bf16[512,256]{1,0:T(8,128)(2,1)} %constant.8.clone.t4_ref), custom_call_target="tpu_custom_call" | custom-call | tf_op jit(solution)/shard_map/patch_flow/pallas_call | solution.py:491
  37.7 1.2 %place.1 = (f32[1,1,2,32]{3,2,1,0:T(2,128)}, f32[1,1,32]{2,1,0:T(1,128)}) custom-call(f32[1,8,128]{2,1,0:T(8,128)} %patch_flow.1.in_ref), custom_call_target="tpu_custom_call" | custom-call | tf_op jit(solution)/shard_map/place/pallas_call | solution.py:516
